TPU v7x, 32 devices: a whole 2x2x4 slice. The times are simulated.
32 devices in a mesh: aux: 8 (over z, x), occ: 4 (over y, core).
Axes of the slice: x: 2, y: 2, z: 4, core: 2. Of those that a mesh axis runs over, the one named last changes fastest.
Arguments:
- factors: bfloat16 [3840, 8, 2560], P('aux', 'occ'), may hold values from -0.25 to 0.25
- pair_list: int32 [4, 2], replicated, may hold values from 0 to 3
- eps_occ: float32 [8], replicated, may hold values from -2 to -0.3
- eps_virt: float32 [2560], replicated, may hold values from 0.2 to 3
Outputs:
- energy_by_virtual: float32 [4, 4, 2560], P('occ', None, 'aux')
All inputs are finite; a program needn't handle non-finite values.
Results may differ from a plain program's by a relative error of at most 0.0003.
Values may be sent and summed in bfloat16 or wider, within the bound.
A program may use at most 192 MiB of HBM per device.

v0:
```python
import jax
import jax.numpy as jnp
from jax import lax
from jax.sharding import PartitionSpec as P


def on_device(factors, pair_list, eps_occ, eps_virt):
    local_q = factors.shape[0]
    orb_local = factors.shape[1]
    virt_width = factors.shape[2]
    aux_count = lax.axis_size("aux")
    my_group = lax.axis_index("occ")
    chosen = pair_list[my_group]
    everyone = lax.all_gather(factors, "occ", axis=1, tiled=True)
    first_block = lax.dynamic_slice_in_dim(everyone, chosen[0] * orb_local, orb_local, 1)
    second = lax.dynamic_slice_in_dim(everyone, chosen[1] * orb_local, orb_local, 1)
    picked = jnp.stack([first_block, second], axis=0)
    rows_grid = 2 ** ((aux_count.bit_length() - 1) // 2)
    cols_grid = aux_count // rows_grid
    span_a = virt_width // rows_grid
    span_b = virt_width // cols_grid
    rows_pieces = picked.reshape(2, local_q, orb_local, rows_grid, span_a).transpose(3, 0, 1, 2, 4)
    rows_pieces = jnp.tile(rows_pieces, (cols_grid, 1, 1, 1, 1))
    cols_pieces = picked.reshape(2, local_q, orb_local, cols_grid, span_b).transpose(3, 0, 1, 2, 4)
    cols_pieces = jnp.repeat(cols_pieces, rows_grid, axis=0)
    send_pieces = jnp.concatenate([rows_pieces, cols_pieces], axis=4)
    regrouped = lax.all_to_all(send_pieces, "aux", split_axis=0, concat_axis=2, tiled=True)[0]
    aux_rank = lax.axis_index("aux")
    row_id = aux_rank % rows_grid
    col_id = aux_rank // rows_grid
    contract = (((0,), (0,)), ((), ()))
    direct = lax.dot_general(
        regrouped[0, :, :, :span_a],
        regrouped[1, :, :, span_a:],
        contract,
        preferred_element_type=jnp.float32,
    )
    swapped = lax.dot_general(
        regrouped[1, :, :, :span_a],
        regrouped[0, :, :, span_a:],
        contract,
        preferred_element_type=jnp.float32,
    )
    swapped = swapped.transpose(2, 1, 0, 3)
    virt_rows = lax.dynamic_slice_in_dim(eps_virt, row_id * span_a, span_a)
    virt_cols = lax.dynamic_slice_in_dim(eps_virt, col_id * span_b, span_b)
    occ_left = lax.dynamic_slice_in_dim(eps_occ, chosen[0] * orb_local, orb_local)
    occ_right = lax.dynamic_slice_in_dim(eps_occ, chosen[1] * orb_local, orb_local)
    denominator = (
        virt_rows[None, :, None, None]
        + virt_cols[None, None, None, :]
        - occ_left[:, None, None, None]
        - occ_right[None, None, :, None]
    )
    partial_value = -jnp.sum(direct * (2.0 * direct - swapped) / denominator, axis=3)
    partial_value = partial_value.transpose(0, 2, 1).reshape(orb_local * orb_local, span_a)
    spread = lax.dynamic_update_slice_in_dim(
        jnp.zeros((orb_local * orb_local, virt_width), jnp.float32),
        partial_value,
        row_id * span_a,
        1,
    )
    shares = lax.psum_scatter(spread, "aux", scatter_dimension=1, tiled=True)
    return shares.reshape(1, orb_local * orb_local, -1)


def solution(mesh):
    return jax.shard_map(
        on_device,
        mesh=mesh,
        in_specs=(P("aux", "occ", None), P(), P(), P()),
        out_specs=P("occ", None, "aux"),
        check_vma=False,
    )
```

profile of v0, /device:TPU:1, one launch (start us, length us, event | category | flops | bytes accessed | tf_op | source)
XLA Modules:
  0.0 1753.9 jit_solution(5238254481175396144)
XLA Ops:
  6.5 5.3 copy.18
  11.9 0.0 all-gather.2.cloned.1.call-update
  11.9 0.1 constant_dynamic-slice_fusion.2
  12.0 0.6 fusion.5
  13.9 125.0 %all-gather.2.cloned.1.call-done = bf16[480,8,2560]{2,0,1:T(8,128)(2,1)} async-done(((bf16[480,2,2560]{2,0,1:T(8,128)(2,1)}), bf16[480,8,2560]{2,0,1:T(8,128)(2,1)}) %all-gather.2.cloned.1.call-update) | async-done | bytes 19660816 | tf_op jit(solution)/shard_map/all_gather | solution.py:14
  138.9 8.2 constant_dynamic-slice_fusion.1
  147.1 10.9 stack.15
  158.1 9.3 stack.18
  167.4 10.9 stack.16
  178.3 9.3 stack.19
  187.6 17.2 maximum_bitcast_fusion
  204.8 9.0 copy.19
  213.7 9.9 maximum_bitcast_fusion.1
  223.6 9.0 copy.20
  232.6 18.7 %tile.4 = bf16[4,2,2,480,2,1280]{5,3,4,2,1,0:T(8,128)(2,1)} broadcast(bf16[2,2,480,2,1280]{4,2,3,1,0:T(8,128)(2,1)} %copy.19), dimensions={1,2,3,4,5} | broadcast | bytes 49152000 | tf_op jit(solution)/shard_map/tile | solution.py:23
  251.3 8.3 broadcast_in_dim.5
  259.6 39.1 %pad_maximum_fusion = bf16[8,2,480,2,1920]{4,2,3,1,0:T(8,128)(2,1)} fusion(bf16[8,2,480,2,640]{4,2,3,1,0:T(8,128)(2,1)} %bitcast.62, bf16[8,2,480,2,1280]{4,2,3,1,0:T(8,128)(2,1)} %bitcast.61), kind=kLoop, calls=%fused_computation | loop fusion | flops 117964800 | bytes 117964800 | tf_op jit(solution)/shard_map/concatenate | solution.py:26
  298.7 9.2 all-to-all-start
  308.0 0.0 reduce-scatter.4.cloned.1.call-start
  308.0 0.1 dynamic_slice.24
  308.1 0.1 dynamic_slice.25
  308.2 0.1 fusion.6
  308.3 0.3 broadcast_add_fusion
  308.6 3.2 broadcast_subtract_fusion
  311.8 1263.4 %all-to-all-done = bf16[8,2,480,2,1920]{4,2,3,1,0:T(8,128)(2,1)} async-done(((bf16[8,2,480,2,1920]{4,2,3,1,0:T(8,128)(2,1)}), bf16[8,2,480,2,1920]{4,2,3,1,0:T(8,128)(2,1)}, u32[]{:S(2)}, u32[]{:S(2)}) %all-to-all-start) | async-done | bytes 58982432 | tf_op jit(solution)/shard_map/all_to_all | solution.py:27
  1575.1 38.9 %copy.21 = bf16[1,2,8,480,2,1920]{5,3,2,4,1,0:T(8,128)(2,1)} copy(bf16[1,2,8,480,2,1920]{5,3,4,1,2,0:T(8,128)(2,1)} %bitcast.7) | data formatting | bytes 117964800 | tf_op jit(solution)/shard_map/all_to_all | solution.py:27
  1614.0 33.4 %fusion = f32[2,1280,2,640]{1,3,0,2:T(8,128)} fusion(bf16[2,3840,2,1920]{3,1,2,0:T(8,128)(2,1)} %bitcast.63), kind=kOutput, calls=%fused_computation.2 | convolution fusion | flops 25165824000 | bytes 42598400 | tf_op jit(solution)/shard_map/dot_general | solution.py:38
  1647.5 35.0 %fusion.4 = f32[2,1280,2]{1,2,0:T(2,128)S(1)} fusion(f32[2]{0:T(128)S(1)} %get-tuple-element.10, f32[2,1280,640]{1,2,0:T(8,128)} %broadcast_subtract_fusion, f32[2,1280,2,640]{1,3,0,2:T(8,128)} %fusion, bf16[2,3840,2,1920]{3,1,2,0:T(8,128)(2,1)} %bitcast.64), kind=kOutput, calls=%fused_computation.13 | convolution fusion | flops 25185480704 | bytes 49172488 | tf_op jit(solution)/shard_map/dot_general | solution.py:32
  1682.5 1.5 copy.26
  1684.1 0.0 reduce-scatter.4.cloned.1.call-update
  1684.1 61.3 %reduce-scatter.4.cloned.1.call-done = f32[320,4]{1,0:T(8,128)} async-done(((f32[2560,4]{1,0:T(8,128)}), f32[320,4]{1,0:T(8,128)}) %reduce-scatter.4.cloned.1.call-update) | async-done | bytes 5136
  1745.4 1.6 copy.27
  (15 shorter events, 0.1 us)
Async XLA Ops:
  6.5 5.4 copy-start
  6.5 132.4 %all-gather.2.cloned.1.call-start = ((), (), s32[]{:S(2)}) async-start(), calls=%async_computation.2 | async-start | bytes 24576000 | tf_op jit(solution)/shard_map/all_gather | solution.py:14
  232.6 18.7 %copy-start.2 = (bf16[4,2,480,2,640]{4,2,3,1,0:T(8,128)(2,1)S(1)}, bf16[4,2,480,2,640]{4,2,3,1,0:T(8,128)(2,1)}, u32[]{:S(2)}) copy-start(bf16[4,2,480,2,640]{4,2,3,1,0:T(8,128)(2,1)} %copy.20) | copy-start | bytes 29491204
  298.7 9.3 copy-start.3
  298.7 9.5 copy-start.4
  298.7 1276.4 %all-to-all-start = ((bf16[8,2,480,2,1920]{4,2,3,1,0:T(8,128)(2,1)}), bf16[8,2,480,2,1920]{4,2,3,1,0:T(8,128)(2,1)}, u32[]{:S(2)}, u32[]{:S(2)}) async-start(bf16[8,2,480,2,1920]{4,2,3,1,0:T(8,128)(2,1)} %pad_maximum_fusion), calls=%async_computation | async-start | bytes 117964800 | tf_op jit(solution)/shard_map/all_to_all | solution.py:27
  308.0 1437.5 %reduce-scatter.4.cloned.1.call-start = ((), (), s32[]{:S(2)}) async-start(), calls=%async_computation.3 | async-start | bytes 1474560
  1647.5 99.6 %copy-start.1 = (s32[4,2]{0,1:T(2,128)S(1)}, s32[4,2]{0,1:T(2,128)}, u32[]{:S(2)}) copy-start(s32[4,2]{0,1:T(2,128)} %param.5) | copy-start | bytes 100
Sparse Core Ops, SparseCore 0:
  12.0 126.8 all-gather.1
  1684.2 61.1 reduce-scatter.3
where the time goes:
time: 1760 us; the launch traced here: 1750 us
  waiting for transfers between devices  1450 us (82%)
  local copies, waits for them, and re-layouts  142 us (8%)
  other arithmetic  69.6 us (4%)
  matrix products  68.4 us (4%)
    all_to_all x1, waiting for transfers between devices, on_device(): lax.all_to_all(send_pieces, 'aux', split_axis=0, concat_axis=2, tiled=True)  1260 us
    all_gather x1, waiting for transfers between devices, on_device(): everyone = lax.all_gather(factors, 'occ', axis=1, tiled=True)  125 us
    unnamed x3, waiting for transfers between devices  61.4 us
    another operation x4, local copies, waits for them, and re-layouts, on_device(): picked = jnp.stack([first_block, second], axis=0)  40.5 us
    concatenate x1, other arithmetic, on_device(): send_pieces = jnp.concatenate([rows_pieces, cols_pieces], axis=4)  39.1 us
    all_to_all x1, local copies, waits for them, and re-layouts, on_device(): lax.all_to_all(send_pieces, 'aux', split_axis=0, concat_axis=2, tiled=True)  38.9 us
  transfers between devices with their start and end apart: 3, of which 3 were waited for; matrix products, arithmetic and copies ran while one was open for 0% of the time, Pallas kernels for 0%

commit v1 on v0

--- a/solution.py
+++ b/solution.py
@@ -1,13 +1,233 @@
+import functools
+
 import jax
 import jax.numpy as jnp
 from jax import lax
+from jax.experimental import pallas as pl
+from jax.experimental.pallas import tpu as pltpu
 from jax.sharding import PartitionSpec as P
 
-
-def on_device(factors, pair_list, eps_occ, eps_virt):
-    local_q = factors.shape[0]
-    orb_local = factors.shape[1]
-    virt_width = factors.shape[2]
+MESH = pl.DeviceIdType.MESH
+
+
+def flip(z, k):
+    return (z // 2 + k // 2) % 2 * 2 + (z + k) % 2
+
+
+def route(planes, slices, sel, gath, zbuf, z_send, z_recv, hop_send, hop_recv, core_send, core_recv):
+    depth, width = sel.shape[3], sel.shape[4]
+    rows = depth // slices
+    steps = planes * slices
+    aux = lax.axis_index("aux")
+    occ = lax.axis_index("occ")
+    z, x, y, c = aux // 2, aux % 2, occ // 2, occ % 2
+
+    def device(z_, x_, y_, c_):
+        return {"aux": z_ * 2 + x_, "occ": y_ * 2 + c_}
+
+    partners = [device(flip(z, k), x, y, c) for k in range(1, planes)]
+    partners += [device(z, 1 - x, y, c), device(z, x, 1 - y, c), device(z, x, y, 1 - c)]
+    barrier = pltpu.get_barrier_semaphore()
+    for partner in partners:
+        pl.semaphore_signal(barrier, inc=1, device_id=partner, device_id_type=MESH)
+    pl.semaphore_wait(barrier, len(partners))
+
+    def span(t):
+        return pl.ds(pl.multiple_of(t * rows, 16), rows)
+
+    def place(s, zs, xs, ys, cs, t):
+        first = pl.multiple_of((zs * 2 + xs) * depth + t * rows, 16)
+        left = pl.multiple_of((ys * 2 + cs) * width, 128)
+        return gath.at[s, pl.ds(first, rows), pl.ds(left, width)]
+
+    def z_copy(t, k, s, rel):
+        zt = flip(z, k)
+        own = x if s == 0 else y
+        w = own if rel == 0 else 1 - own
+        dst = place(s, z, x, y, c, t) if rel == 0 else zbuf.at[k, s, span(t), :]
+        return pltpu.make_async_remote_copy(
+            src_ref=sel.at[zt, s, w, span(t), :],
+            dst_ref=dst,
+            send_sem=z_send.at[t, k, s, rel],
+            recv_sem=z_recv.at[t, k, s, rel],
+            device_id=device(zt, x, y, c),
+            device_id_type=MESH,
+        )
+
+    def z_keep(t, s, rel):
+        own = x if s == 0 else y
+        w = own if rel == 0 else 1 - own
+        dst = place(s, z, x, y, c, t) if rel == 0 else zbuf.at[0, s, span(t), :]
+        return pltpu.make_async_copy(sel.at[z, s, w, span(t), :], dst, z_recv.at[t, 0, s, rel])
+
+    def hop(n, s, kind):
+        t, k = n // planes, n % planes
+        zs = flip(z, k)
+        share = device(z, x, 1 - y, c) if s == 0 else device(z, 1 - x, y, c)
+        other = device(z, 1 - x, y, c) if s == 0 else device(z, x, 1 - y, c)
+        xs, ys = (1 - x, y) if s == 0 else (x, 1 - y)
+        mine = place(s, zs, x, y, c, t)
+        if kind == 0:
+            src, dst, target = mine, mine, share
+        elif kind == 1:
+            src, dst, target = zbuf.at[k, s, span(t), :], mine, other
+        else:
+            src = place(s, zs, xs, ys, c, t)
+            dst, target = src, share
+        return pltpu.make_async_remote_copy(
+            src_ref=src,
+            dst_ref=dst,
+            send_sem=hop_send.at[n, s, kind],
+            recv_sem=hop_recv.at[n, s, kind],
+            device_id=target,
+            device_id_type=MESH,
+        )
+
+    def across(n, s, kind):
+        t, k = n // planes, n % planes
+        zs = flip(z, k)
+        if s == 0:
+            spots = [(x, y), (x, 1 - y), (1 - x, y), (1 - x, 1 - y)]
+        else:
+            spots = [(x, y), (1 - x, y), (x, 1 - y), (1 - x, 1 - y)]
+        ref = place(s, zs, spots[kind][0], spots[kind][1], c, t)
+        return pltpu.make_async_remote_copy(
+            src_ref=ref,
+            dst_ref=ref,
+            send_sem=core_send.at[n, s, kind],
+            recv_sem=core_recv.at[n, s, kind],
+            device_id=device(z, x, y, 1 - c),
+            device_id_type=MESH,
+        )
+
+    @pl.loop(0, slices)
+    def _(t):
+        for s in range(2):
+            for rel in (1, 0):
+                z_keep(t, s, rel).start()
+                for k in (2, 3, 1):
+                    z_copy(t, k, s, rel).start()
+
+    @pl.loop(0, steps + 2)
+    def _(n):
+        @pl.when(n < steps)
+        def _():
+            t, k = n // planes, n % planes
+            for s in range(2):
+                for rel in (1, 0):
+
+                    @pl.when(k == 0)
+                    def _():
+                        z_keep(t, s, rel).wait()
+
+                    @pl.when(k > 0)
+                    def _():
+                        z_copy(t, k, s, rel).wait_recv()
+
+                    hop(n, s, rel).start()
+                    if rel == 0:
+                        across(n, s, 0).start()
+
+        @pl.when((n >= 1) & (n < steps + 1))
+        def _():
+            for s in range(2):
+                hop(n - 1, s, 1).wait_recv()
+                hop(n - 1, s, 2).start()
+                across(n - 1, s, 2).start()
+
+        @pl.when(n >= 2)
+        def _():
+            for s in range(2):
+                hop(n - 2, s, 0).wait_recv()
+                across(n - 2, s, 1).start()
+                hop(n - 2, s, 2).wait_recv()
+                across(n - 2, s, 3).start()
+
+    @pl.loop(0, slices)
+    def _(t):
+        for s in range(2):
+            for rel in (1, 0):
+                for k in (2, 3, 1):
+                    z_copy(t, k, s, rel).wait_send()
+
+    @pl.loop(0, steps)
+    def _(n):
+        for s in range(2):
+            for kind in range(3):
+                hop(n, s, kind).wait_send()
+            for kind in range(4):
+                across(n, s, kind).wait()
+
+
+def by_planes(factors, pair_list, eps_occ, eps_virt):
+    local_q, orb_local, virt = factors.shape
+    n_aux = lax.axis_size("aux")
+    n_occ = lax.axis_size("occ")
+    planes = pair_list.shape[0]
+    width = virt // n_occ
+    slices = 3 if local_q % 48 == 0 else 1
+    steps = planes * slices
+    aux = lax.axis_index("aux")
+    occ = lax.axis_index("occ")
+    z, x, y, c = aux // 2, aux % 2, occ // 2, occ % 2
+
+    mine = factors.transpose(1, 0, 2)
+    quarter = lax.all_to_all(mine, "occ", split_axis=2, concat_axis=0, tiled=True)
+    blocks = quarter.reshape(n_occ, orb_local, local_q, width)
+    sel = jnp.concatenate(
+        [lax.dynamic_slice_in_dim(blocks, pair_list[p, s], 1, 0) for p in range(planes) for s in range(2)], axis=0
+    ).reshape(planes, 2, orb_local, local_q, width)
+
+    gath, _ = pl.pallas_call(
+        functools.partial(route, planes, slices),
+        out_shape=[
+            jax.ShapeDtypeStruct((2, n_aux * local_q, virt), factors.dtype),
+            jax.ShapeDtypeStruct((planes, 2, local_q, width), factors.dtype),
+        ],
+        in_specs=[pl.BlockSpec(memory_space=pl.ANY)],
+        out_specs=[pl.BlockSpec(memory_space=pl.ANY)] * 2,
+        scratch_shapes=[
+            pltpu.SemaphoreType.DMA((slices, planes, 2, 2)),
+            pltpu.SemaphoreType.DMA((slices, planes, 2, 2)),
+            pltpu.SemaphoreType.DMA((steps, 2, 3)),
+            pltpu.SemaphoreType.DMA((steps, 2, 3)),
+            pltpu.SemaphoreType.DMA((steps, 2, 4)),
+            pltpu.SemaphoreType.DMA((steps, 2, 4)),
+        ],
+        compiler_params=pltpu.CompilerParams(collective_id=0, has_side_effects=True),
+    )(sel)
+
+    half = virt // 2
+    chosen = lax.dynamic_index_in_dim(pair_list, z, 0, keepdims=False)
+    e_i = lax.dynamic_index_in_dim(eps_occ, chosen[0] * orb_local + x, 0, keepdims=False)
+    e_j = lax.dynamic_index_in_dim(eps_occ, chosen[1] * orb_local + y, 0, keepdims=False)
+    contract = (((0,), (0,)), ((), ()))
+    tiles = []
+    for t in range(2):
+        t_col = (t + c) % 2
+        cols = lax.dynamic_slice_in_dim(gath[1], t_col * half, half, 1)
+        tiles.append(
+            lax.dot_general(gath[0, :, t * half : (t + 1) * half], cols, contract, preferred_element_type=jnp.float32)
+        )
+    sums = []
+    for t in range(2):
+        t_col = (t + c) % 2
+        swapped = jnp.where(c == 0, tiles[t], tiles[1 - t]).T
+        rows_e = eps_virt[t * half : (t + 1) * half]
+        cols_e = lax.dynamic_slice_in_dim(eps_virt, t_col * half, half)
+        denominator = rows_e[:, None] + cols_e[None, :] - e_i - e_j
+        sums.append(-jnp.sum(tiles[t] * (2.0 * tiles[t] - swapped) / denominator, axis=1))
+    part = jnp.concatenate(sums)
+
+    spread = lax.all_to_all(part.reshape(n_aux, virt // n_aux), "aux", split_axis=0, concat_axis=0, tiled=True)
+    every = lax.all_gather(spread, "occ", axis=0, tiled=False)
+    every = every.reshape(2, 2, planes, 2, virt // n_aux).sum(axis=1)
+    own = lax.dynamic_index_in_dim(every, occ, 1, keepdims=False)
+    return own.transpose(1, 0, 2).reshape(1, 4, virt // n_aux)
+
+
+def by_groups(factors, pair_list, eps_occ, eps_virt):
+    local_q, orb_local, virt_width = factors.shape
     aux_count = lax.axis_size("aux")
     my_group = lax.axis_index("occ")
     chosen = pair_list[my_group]
@@ -30,16 +250,10 @@
     col_id = aux_rank // rows_grid
     contract = (((0,), (0,)), ((), ()))
     direct = lax.dot_general(
-        regrouped[0, :, :, :span_a],
-        regrouped[1, :, :, span_a:],
-        contract,
-        preferred_element_type=jnp.float32,
+        regrouped[0, :, :, :span_a], regrouped[1, :, :, span_a:], contract, preferred_element_type=jnp.float32
     )
     swapped = lax.dot_general(
-        regrouped[1, :, :, :span_a],
-        regrouped[0, :, :, span_a:],
-        contract,
-        preferred_element_type=jnp.float32,
+        regrouped[1, :, :, :span_a], regrouped[0, :, :, span_a:], contract, preferred_element_type=jnp.float32
     )
     swapped = swapped.transpose(2, 1, 0, 3)
     virt_rows = lax.dynamic_slice_in_dim(eps_virt, row_id * span_a, span_a)
@@ -55,16 +269,26 @@
     partial_value = -jnp.sum(direct * (2.0 * direct - swapped) / denominator, axis=3)
     partial_value = partial_value.transpose(0, 2, 1).reshape(orb_local * orb_local, span_a)
     spread = lax.dynamic_update_slice_in_dim(
-        jnp.zeros((orb_local * orb_local, virt_width), jnp.float32),
-        partial_value,
-        row_id * span_a,
-        1,
+        jnp.zeros((orb_local * orb_local, virt_width), jnp.float32), partial_value, row_id * span_a, 1
     )
     shares = lax.psum_scatter(spread, "aux", scatter_dimension=1, tiled=True)
     return shares.reshape(1, orb_local * orb_local, -1)
 
 
 def solution(mesh):
+    def on_device(factors, pair_list, eps_occ, eps_virt):
+        planes = pair_list.shape[0]
+        fits = (
+            mesh.shape["aux"] == 2 * planes
+            and mesh.shape["occ"] == 4
+            and planes == 4
+            and factors.shape[1] == 2
+            and factors.shape[0] % 16 == 0
+            and factors.shape[2] % 512 == 0
+        )
+        body = by_planes if fits else by_groups
+        return body(factors, pair_list, eps_occ, eps_virt)
+
     return jax.shard_map(
         on_device,
         mesh=mesh,

time: 1760 us -> 509 us (0.29)
  waiting for transfers between devices: 1450 us -> 46.1 us
  Pallas kernels: 0 us -> 264 us
  other arithmetic: 69.6 us -> 12.3 us
  local copies, waits for them, and re-layouts: 142 us -> 112 us
  matrix products: 68.4 us -> 40.6 us
    all_to_all x1 -> x2, waiting for transfers between devices: 1260 us -> 46.1 us  [the longest x1 40.7 us: by_planes(): lax.all_to_all(mine, 'occ', split_axis=2, concat_axis=0, tiled=True)]
    pallas_call x0 -> x1, Pallas kernels: none -> 264 us  [by_planes(): pl.pallas_call(functools.partial(route, planes, slices), out_shape=[jax.S...]
    all_gather x1 -> x0, waiting for transfers between devices: 125 us -> none  [on_device(): everyone = lax.all_gather(factors, 'occ', axis=1, tiled=True)]
    unnamed x3 -> x0, waiting for transfers between devices: 61.4 us -> none
    concatenate x1, other arithmetic: 39.1 us -> 0.01 us  [by_planes(): part = jnp.concatenate(sums)]
    all_to_all x1, local copies, waits for them, and re-layouts: 38.9 us -> 0.61 us  [by_planes(): lax.all_to_all(part.reshape(n_aux, virt // n_aux), 'aux', split_axis=0, c...]
    dot_general x2, matrix products: 68.4 us -> 40.6 us  [by_planes(): lax.dot_general(gath[0, :, t * half:(t + 1) * half], cols, contract, pref...]
    transpose x2 -> x0, other arithmetic: 27 us -> none  [the longest x1 17.2 us: on_device(): picked.reshape(2, local_q, orb_local, rows_grid, span_a)]
  transfers between devices with their start and end apart: 3 -> 2, of which waited for: 3 -> 2; matrix products, arithmetic and copies ran while one was open for 0% -> 0% of each run, Pallas kernels for 0% -> 0%
where the time goes in v1:
time: 509 us; the launch traced here: 506 us
  Pallas kernels  264 us (52%)
  local copies, waits for them, and re-layouts  112 us (22%)
  waiting for transfers between devices  46.1 us (9%)
  matrix products  40.6 us (8%)
  between operations  16.2 us (3%)
  other arithmetic  12.3 us (2%)
  starting transfers between devices  8.53 us (2%)
  blocking collectives  6.55 us (1%)
    pallas_call x1, Pallas kernels, by_planes(): pl.pallas_call(functools.partial(route, planes, slices), out_shape=[jax.S...  264 us
    another operation x9, local copies, waits for them, and re-layouts  43.5 us
    all_to_all x1, waiting for transfers between devices, by_planes(): lax.all_to_all(mine, 'occ', split_axis=2, concat_axis=0, tiled=True)  40.7 us
    dot_general x2, matrix products, by_planes(): lax.dot_general(gath[0, :, t * half:(t + 1) * half], cols, contract, pref...  40.6 us
    unnamed x24, local copies, waits for them, and re-layouts  31 us
    slice x1, local copies, waits for them, and re-layouts, by_planes(): cols = lax.dynamic_slice_in_dim(gath[1], t_col * half, half, 1)  16.4 us
    dot_general x2, local copies, waits for them, and re-layouts, by_planes(): lax.dot_general(gath[0, :, t * half:(t + 1) * half], cols, contract, pref...  16.3 us
    reduce_sum x1, other arithmetic, by_planes(): jnp.sum(tiles[t] * (2.0 * tiles[t] - swapped) / denominator, axis=1)  12.2 us
  transfers between devices with their start and end apart: 2, of which 2 were waited for; matrix products, arithmetic and copies ran while one was open for 0% of the time, Pallas kernels for 0%

profile of v1, /device:TPU:1, one launch (start us, length us, event | category | flops | bytes accessed | tf_op | source)
XLA Modules:
  0.0 506.4 jit_solution(14761743658281197004)
XLA Ops:
  0.0 18.7 %copy.56 = bf16[480,2,2560]{0,1,2:T(2,128)(2,1)} copy(bf16[480,2,2560]{2,1,0:T(2,128)(2,1)} %param.4) | data formatting | bytes 9830400 | tf_op args[0]
  18.7 5.2 %all-to-all-start = ((bf16[2,480,2560]{1,0,2:T(2,128)(2,1)}), bf16[2,480,2560]{1,0,2:T(2,128)(2,1)}, u32[]{:S(2)}, u32[]{:S(2)}) async-start(bf16[2,480,2560]{1,0,2:T(2,128)(2,1)} %bitcast.63), calls=%async_computation | async-start | bytes 10485760 | tf_op jit(solution)/shard_map/all_to_all | solution.py:175
  26.0 0.7 fusion.20
  41.3 0.6 fusion.21
  42.0 40.7 %all-to-all-done = bf16[2,480,2560]{1,0,2:T(2,128)(2,1)} async-done(((bf16[2,480,2560]{1,0,2:T(2,128)(2,1)}), bf16[2,480,2560]{1,0,2:T(2,128)(2,1)}, u32[]{:S(2)}, u32[]{:S(2)}) %all-to-all-start) | async-done | bytes 4915232 | tf_op jit(solution)/shard_map/all_to_all | solution.py:175
  82.7 12.2 %constant_dynamic-slice_fusion.1 = (bf16[2,480,1,640]{1,0,3,2:T(2,128)(2,1)}, bf16[2,480,1,640]{1,0,3,2:T(2,128)(2,1)}, bf16[2,480,1,640]{1,0,3,2:T(2,128)(2,1)}...) fusion(bf16[2,480,4,640]{1,0,3,2:T(2,128)(2,1)} %bitcast.1, ...), kind=kLoop, calls=%fused_computation.31 | loop fusion | bytes 19660832 | tf_op jit(solution)/shard_map/dynamic-slice.7
  95.0 4.3 copy.64
  99.3 4.3 copy.63
  103.6 4.3 copy.62
  107.9 4.3 copy.61
  112.2 4.3 copy.60
  116.5 4.3 copy.59
  120.7 2.8 copy.58
  123.5 2.8 copy.57
  126.3 2.6 bitcast_dynamic-update-slice_fusion.7
  128.9 2.5 bitcast_dynamic-update-slice_fusion.6
  131.4 2.5 bitcast_dynamic-update-slice_fusion.5
  133.9 1.2 bitcast_dynamic-update-slice_fusion.4
  135.1 1.1 bitcast_dynamic-update-slice_fusion.3
  136.3 1.2 bitcast_dynamic-update-slice_fusion.2
  137.4 1.2 bitcast_dynamic-update-slice_fusion.1
  138.6 1.2 bitcast_dynamic-update-slice_fusion
  139.8 264.3 %shard_map.46 = (bf16[2,3840,2560]{2,1,0:T(8,128)(2,1)}, bf16[4,2,480,640]{3,2,1,0:T(8,128)(2,1)}) custom-call(bf16[4,2,2,480,640]{4,3,2,1,0:T(8,128)(2,1)} %bitcast.18.sel), custom_call_target="tpu_custom_call" | custom-call | tf_op jit(solution)/shard_map/pallas_call | solution.py:181
  404.1 16.4 %slice.57 = bf16[1,3840,2560]{2,1,0:T(8,128)(2,1)} slice(bf16[2,3840,2560]{2,1,0:T(8,128)(2,1)} %get-tuple-element.6), slice={[1:2], [0:3840], [0:2560]} | slice | bytes 39321600 | tf_op jit(solution)/shard_map/slice | solution.py:208
  420.4 20.3 %fusion = f32[1280,1280]{1,0:T(8,128)} fusion(bf16[1,3840,2560]{2,1,0:T(8,128)(2,1)} %slice.57, s32[]{:T(128)S(6)} %select_n.110, bf16[2,3840,2560]{2,1,0:T(8,128)(2,1)} %get-tuple-element.6), kind=kOutput, calls=%fused_computation | convolution fusion | flops 12582912000 | bytes 26214404 | tf_op jit(solution)/shard_map/dot_general | solution.py:210
  440.8 20.3 %fusion.3 = f32[1280,1280]{1,0:T(8,128)} fusion(bf16[1,3840,2560]{2,1,0:T(8,128)(2,1)} %slice.57, s32[]{:T(128)S(6)} %select_n.107, bf16[2,3840,2560]{2,1,0:T(8,128)(2,1)} %get-tuple-element.6), kind=kOutput, calls=%fused_computation.3 | convolution fusion | flops 12582912000 | bytes 26214404 | tf_op jit(solution)/shard_map/dot_general | solution.py:210
  461.1 8.2 %copy.66 = f32[1280,1280]{0,1:T(8,128)} copy(f32[1280,1280]{1,0:T(8,128)} %fusion.3) | data formatting | bytes 13107200 | tf_op jit(solution)/shard_map/dot_general | solution.py:210
  469.2 8.2 %copy.68 = f32[1280,1280]{0,1:T(8,128)} copy(f32[1280,1280]{1,0:T(8,128)} %fusion) | data formatting | bytes 13107200 | tf_op jit(solution)/shard_map/dot_general | solution.py:210
  477.4 12.2 %fusion.14 = (f32[1280]{0:T(1024)S(1)}, f32[1280]{0:T(1024)S(1)}) fusion(f32[1280,1280]{0,1:T(8,128)} %copy.66, f32[1280,1280]{1,0:T(8,128)} %fusion.3, f32[1280,1280]{1,0:T(8,128)} %fusion, f32[]{:T(128)} %bitcast.27, f32[]{:T(128)} %bitcast.25, f32[1280]{0:T(1024)S(1)} %get-tuple-element.18, f32[1280]{0:T(1024)S(1)} %get-tuple-element.19, pred[]{:T(512)S(6)} %eq.11, ...), kind=kLoop, calls=%fused_computation.16 | loop fusion | flops 29488640 | bytes 26245128 | tf_op jit(solution)/shard_map/reduce_sum | solution.py:219
  490.4 3.3 all-to-all-start.1
  493.7 5.3 %all-to-all-done.1 = f32[8,1,320]{2,1,0:T(1,128)S(1)} async-done(((f32[8,1,320]{2,1,0:T(1,128)}), f32[8,1,320]{2,1,0:T(1,128)S(1)}, u32[]{:S(2)}, u32[]{:S(2)}) %all-to-all-start.1) | async-done | bytes 10272 | tf_op jit(solution)/shard_map/all_to_all | solution.py:222
  499.1 6.5 %all-gather = f32[32,1,320]{2,1,0:T(1,128)S(1)} all-gather(f32[8,1,320]{2,1,0:T(1,128)S(1)} %all-to-all-done.1), channel_id=2, replica_groups=mesh['aux'=8,'occ'=4] {'occ'}, dimensions={0}, use_global_device_ids=true | all-gather | bytes 51200 | tf_op jit(solution)/shard_map/all_gather | solution.py:223
  (31 shorter events, 2.4 us)
Async XLA Ops:
  18.7 5.3 %copy-start.6 = (s32[4,2]{0,1:T(2,128)S(1)}, s32[4,2]{0,1:T(2,128)}, u32[]{:S(2)}) copy-start(s32[4,2]{0,1:T(2,128)} %param.5) | copy-start | bytes 100
  18.7 22.6 %copy-start.7 = (f32[8]{0:T(128)S(1)}, f32[8]{0:T(128)}, u32[]{:S(2)}) copy-start(f32[8]{0:T(128)} %param.6) | copy-start | bytes 100
  18.7 23.3 %copy-start.5 = (f32[2560]{0:T(1024)S(1)}, f32[2560]{0:T(1024)}, u32[]{:S(2)}) copy-start(f32[2560]{0:T(1024)} %param.7) | copy-start | bytes 30724
  18.7 64.1 %all-to-all-start = ((bf16[2,480,2560]{1,0,2:T(2,128)(2,1)}), bf16[2,480,2560]{1,0,2:T(2,128)(2,1)}, u32[]{:S(2)}, u32[]{:S(2)}) async-start(bf16[2,480,2560]{1,0,2:T(2,128)(2,1)} %bitcast.63), calls=%async_computation | async-start | bytes 10485760 | tf_op jit(solution)/shard_map/all_to_all | solution.py:175
  123.5 11.6 %copy-start.3 = (bf16[2,480,1,640]{3,1,0,2:T(8,128)(2,1)S(1)}, bf16[2,480,1,640]{3,1,0,2:T(8,128)(2,1)}, u32[]{:S(2)}) copy-start(bf16[2,480,1,640]{3,1,0,2:T(8,128)(2,1)} %copy.61) | copy-start | bytes 3686404
  126.3 7.7 %copy-start.4 = (bf16[2,480,1,640]{3,1,0,2:T(8,128)(2,1)S(1)}, bf16[2,480,1,640]{3,1,0,2:T(8,128)(2,1)}, u32[]{:S(2)}) copy-start(bf16[2,480,1,640]{3,1,0,2:T(8,128)(2,1)} %copy.60) | copy-start | bytes 3686404
  126.3 10.0 %copy-start.2 = (bf16[2,480,1,640]{3,1,0,2:T(8,128)(2,1)S(1)}, bf16[2,480,1,640]{3,1,0,2:T(8,128)(2,1)}, u32[]{:S(2)}) copy-start(bf16[2,480,1,640]{3,1,0,2:T(8,128)(2,1)} %copy.62) | copy-start | bytes 3686404
  128.9 8.5 %copy-start.1 = (bf16[2,480,1,640]{3,1,0,2:T(8,128)(2,1)S(1)}, bf16[2,480,1,640]{3,1,0,2:T(8,128)(2,1)}, u32[]{:S(2)}) copy-start(bf16[2,480,1,640]{3,1,0,2:T(8,128)(2,1)} %copy.63) | copy-start | bytes 3686404
  131.4 7.2 %copy-start = (bf16[2,480,1,640]{3,1,0,2:T(8,128)(2,1)S(1)}, bf16[2,480,1,640]{3,1,0,2:T(8,128)(2,1)}, u32[]{:S(2)}) copy-start(bf16[2,480,1,640]{3,1,0,2:T(8,128)(2,1)} %copy.64) | copy-start | bytes 3686404
  490.4 8.7 %all-to-all-start.1 = ((f32[8,1,320]{2,1,0:T(1,128)}), f32[8,1,320]{2,1,0:T(1,128)S(1)}, u32[]{:S(2)}, u32[]{:S(2)}) async-start(f32[8,1,320]{2,1,0:T(1,128)} %all_to_all.17), calls=%async_computation.1 | async-start | bytes 24576 | tf_op jit(solution)/shard_map/all_to_all | solution.py:222

commit v2 on v1

--- a/solution.py
+++ b/solution.py
@@ -14,9 +14,14 @@
     return (z // 2 + k // 2) % 2 * 2 + (z + k) % 2
 
 
-def route(planes, slices, sel, gath, zbuf, z_send, z_recv, hop_send, hop_recv, core_send, core_recv):
-    depth, width = sel.shape[3], sel.shape[4]
+def route(
+    planes, slices, pairs, near, far, mine, part, gath, zbuf, quarter, sel, acc, held, turned,
+    o_send, o_recv, z_send, z_recv, hop_send, hop_recv, core_send, core_recv, held_sem,
+):
+    depth, virt = mine.shape[1], mine.shape[2]
     rows = depth // slices
+    width = virt // 4
+    half = virt // 2
     steps = planes * slices
     aux = lax.axis_index("aux")
     occ = lax.axis_index("occ")
@@ -25,8 +30,11 @@
     def device(z_, x_, y_, c_):
         return {"aux": z_ * 2 + x_, "occ": y_ * 2 + c_}
 
+    def fellow(d):
+        return {"aux": aux, "occ": flip(occ, d)}
+
     partners = [device(flip(z, k), x, y, c) for k in range(1, planes)]
-    partners += [device(z, 1 - x, y, c), device(z, x, 1 - y, c), device(z, x, y, 1 - c)]
+    partners += [fellow(d) for d in range(1, 4)] + [device(z, 1 - x, y, c)]
     barrier = pltpu.get_barrier_semaphore()
     for partner in partners:
         pl.semaphore_signal(barrier, inc=1, device_id=partner, device_id_type=MESH)
@@ -39,6 +47,20 @@
         first = pl.multiple_of((zs * 2 + xs) * depth + t * rows, 16)
         left = pl.multiple_of((ys * 2 + cs) * width, 128)
         return gath.at[s, pl.ds(first, rows), pl.ds(left, width)]
+
+    def o_copy(t, d):
+        to = flip(occ, d)
+        src = mine.at[:, pl.ds(t * rows, rows), pl.ds(pl.multiple_of(to * width, 128), width)]
+        if d == 0:
+            return pltpu.make_async_copy(src, quarter[t].at[occ], o_recv.at[t, 0])
+        return pltpu.make_async_remote_copy(
+            src_ref=src,
+            dst_ref=quarter[t].at[occ],
+            send_sem=o_send.at[t, d],
+            recv_sem=o_recv.at[t, d],
+            device_id=fellow(d),
+            device_id_type=MESH,
+        )
 
     def z_copy(t, k, s, rel):
         zt = flip(z, k)
@@ -46,7 +68,7 @@
         w = own if rel == 0 else 1 - own
         dst = place(s, z, x, y, c, t) if rel == 0 else zbuf.at[k, s, span(t), :]
         return pltpu.make_async_remote_copy(
-            src_ref=sel.at[zt, s, w, span(t), :],
+            src_ref=sel.at[t, zt, s, w],
             dst_ref=dst,
             send_sem=z_send.at[t, k, s, rel],
             recv_sem=z_recv.at[t, k, s, rel],
@@ -58,7 +80,7 @@
         own = x if s == 0 else y
         w = own if rel == 0 else 1 - own
         dst = place(s, z, x, y, c, t) if rel == 0 else zbuf.at[0, s, span(t), :]
-        return pltpu.make_async_copy(sel.at[z, s, w, span(t), :], dst, z_recv.at[t, 0, s, rel])
+        return pltpu.make_async_copy(sel.at[t, z, s, w], dst, z_recv.at[t, 0, s, rel])
 
     def hop(n, s, kind):
         t, k = n // planes, n % planes
@@ -66,11 +88,11 @@
         share = device(z, x, 1 - y, c) if s == 0 else device(z, 1 - x, y, c)
         other = device(z, 1 - x, y, c) if s == 0 else device(z, x, 1 - y, c)
         xs, ys = (1 - x, y) if s == 0 else (x, 1 - y)
-        mine = place(s, zs, x, y, c, t)
+        own = place(s, zs, x, y, c, t)
         if kind == 0:
-            src, dst, target = mine, mine, share
+            src, dst, target = own, own, share
         elif kind == 1:
-            src, dst, target = zbuf.at[k, s, span(t), :], mine, other
+            src, dst, target = zbuf.at[k, s, span(t), :], own, other
         else:
             src = place(s, zs, xs, ys, c, t)
             dst, target = src, share
@@ -100,16 +122,56 @@
             device_id_type=MESH,
         )
 
-    @pl.loop(0, slices)
-    def _(t):
+    def fetch(t, s, q):
+        first = pl.multiple_of(q * depth + t * rows, 16)
+        return pltpu.make_async_copy(
+            gath.at[s, pl.ds(first, rows), :],
+            held.at[t % 2, s, pl.ds(q * rows, rows), :],
+            held_sem.at[t % 2, s, q],
+        )
+
+    def start_exchange(t):
+        for d in (2, 3, 1, 0):
+            o_copy(t, d).start()
+
+    def choose(t):
+        for d in (0, 1, 2, 3):
+            if d == 0:
+                o_copy(t, d).wait()
+            else:
+                o_copy(t, d).wait_recv()
+        if t + 2 < slices:
+            start_exchange(t + 2)
+        for p in range(planes):
+            for s in range(2):
+                block = pairs[p, s]
+                for w in range(2):
+                    sel[t, p, s, w] = quarter[t][block, w]
         for s in range(2):
             for rel in (1, 0):
                 z_keep(t, s, rel).start()
                 for k in (2, 3, 1):
                     z_copy(t, k, s, rel).start()
 
-    @pl.loop(0, steps + 2)
+    start_exchange(0)
+    if slices > 1:
+        start_exchange(1)
+
+    @pl.loop(0, 2 * (half // 128))
+    def _(r):
+        tile, blk = r // (half // 128), r % (half // 128)
+        acc[tile, pl.ds(pl.multiple_of(blk * 128, 128), 128), :] = jnp.zeros((128, half), jnp.float32)
+
+    choose(0)
+
+    @pl.loop(0, steps + 8)
     def _(n):
+        for t in range(1, slices):
+
+            @pl.when(n == max(0, planes * t - 6))
+            def _():
+                choose(t)
+
         @pl.when(n < steps)
         def _():
             t, k = n // planes, n % planes
@@ -135,13 +197,64 @@
                 hop(n - 1, s, 2).start()
                 across(n - 1, s, 2).start()
 
-        @pl.when(n >= 2)
+        @pl.when((n >= 2) & (n < steps + 2))
         def _():
             for s in range(2):
                 hop(n - 2, s, 0).wait_recv()
                 across(n - 2, s, 1).start()
                 hop(n - 2, s, 2).wait_recv()
                 across(n - 2, s, 3).start()
+
+        @pl.when((n >= 3) & (n < steps + 3))
+        def _():
+            for s in range(2):
+                for kind in range(4):
+                    across(n - 3, s, kind).wait_recv()
+
+        @pl.when((n >= 6) & (n < steps + 6) & (n % planes == 2))
+        def _():
+            t = (n - 6) // planes
+            for s in range(2):
+                for q in range(2 * planes):
+                    fetch(t, s, q).start()
+
+        @pl.when(n >= 8)
+        def _():
+            t, unit = (n - 8) // planes, n % planes
+
+            @pl.when(unit == 0)
+            def _():
+                for s in range(2):
+                    for q in range(2 * planes):
+                        fetch(t, s, q).wait()
+
+            tile = unit // 2
+            top = pl.multiple_of(unit % 2 * width, 128)
+            left = pl.multiple_of((tile + c) % 2 * half, 128)
+            lhs = pl.multiple_of(tile * half + unit % 2 * width, 128)
+            turned[...] = held[t % 2, 0, :, pl.ds(lhs, width)].T
+
+            @pl.loop(0, half // 256)
+            def _(col):
+                cols = pl.ds(pl.multiple_of(left + col * 256, 128), 256)
+                into = pl.ds(pl.multiple_of(col * 256, 128), 256)
+                acc[tile, pl.ds(top, width), into] += jnp.dot(
+                    turned[...], held[t % 2, 1, :, cols], preferred_element_type=jnp.float32
+                )
+
+    @pl.loop(0, 2 * (half // 128))
+    def _(r):
+        tile, blk = r // (half // 128), r % (half // 128)
+        at = pl.ds(pl.multiple_of(blk * 128, 128), 128)
+        direct = acc[tile, at, :].T
+        swapped = acc[(tile + c) % 2, :, at]
+        denominator = far[tile] + near[tile, :, at]
+        value = direct * (2.0 * direct - swapped) / denominator
+        part[tile, :, at] = -jnp.sum(value, axis=0, keepdims=True)
+
+    for t in range(slices):
+        for d in (1, 2, 3):
+            o_copy(t, d).wait_send()
 
     @pl.loop(0, slices)
     def _(t):
@@ -156,68 +269,68 @@
             for kind in range(3):
                 hop(n, s, kind).wait_send()
             for kind in range(4):
-                across(n, s, kind).wait()
+                across(n, s, kind).wait_send()
 
 
 def by_planes(factors, pair_list, eps_occ, eps_virt):
     local_q, orb_local, virt = factors.shape
     n_aux = lax.axis_size("aux")
-    n_occ = lax.axis_size("occ")
     planes = pair_list.shape[0]
-    width = virt // n_occ
-    slices = 3 if local_q % 48 == 0 else 1
+    width = virt // 4
+    half = virt // 2
+    slices = next(n for n in (5, 3, 2, 1) if local_q % (16 * n) == 0)
+    rows = local_q // slices
     steps = planes * slices
     aux = lax.axis_index("aux")
     occ = lax.axis_index("occ")
     z, x, y, c = aux // 2, aux % 2, occ // 2, occ % 2
 
+    chosen = lax.dynamic_index_in_dim(pair_list, z, 0, keepdims=False)
+    e_i = lax.dynamic_index_in_dim(eps_occ, chosen[0] * orb_local + x, 0, keepdims=False)
+    e_j = lax.dynamic_index_in_dim(eps_occ, chosen[1] * orb_local + y, 0, keepdims=False)
+    halves = eps_virt.reshape(2, half)
+    near = (halves - e_i - e_j).reshape(2, 1, half)
+    far = jnp.where(c == 0, halves, halves[::-1]).reshape(2, half, 1)
     mine = factors.transpose(1, 0, 2)
-    quarter = lax.all_to_all(mine, "occ", split_axis=2, concat_axis=0, tiled=True)
-    blocks = quarter.reshape(n_occ, orb_local, local_q, width)
-    sel = jnp.concatenate(
-        [lax.dynamic_slice_in_dim(blocks, pair_list[p, s], 1, 0) for p in range(planes) for s in range(2)], axis=0
-    ).reshape(planes, 2, orb_local, local_q, width)
-
-    gath, _ = pl.pallas_call(
+
+    part, _, _ = pl.pallas_call(
         functools.partial(route, planes, slices),
         out_shape=[
+            jax.ShapeDtypeStruct((2, 1, half), jnp.float32),
             jax.ShapeDtypeStruct((2, n_aux * local_q, virt), factors.dtype),
             jax.ShapeDtypeStruct((planes, 2, local_q, width), factors.dtype),
         ],
-        in_specs=[pl.BlockSpec(memory_space=pl.ANY)],
-        out_specs=[pl.BlockSpec(memory_space=pl.ANY)] * 2,
+        in_specs=[
+            pl.BlockSpec(memory_space=pltpu.SMEM),
+            pl.BlockSpec(memory_space=pltpu.VMEM),
+            pl.BlockSpec(memory_space=pltpu.VMEM),
+            pl.BlockSpec(memory_space=pl.ANY),
+        ],
+        out_specs=[
+            pl.BlockSpec(memory_space=pltpu.VMEM),
+            pl.BlockSpec(memory_space=pl.ANY),
+            pl.BlockSpec(memory_space=pl.ANY),
+        ],
         scratch_shapes=[
+            [pltpu.VMEM((4, 2, rows, width), factors.dtype) for _ in range(slices)],
+            pltpu.VMEM((slices, planes, 2, 2, rows, width), factors.dtype),
+            pltpu.VMEM((2, half, half), jnp.float32),
+            pltpu.VMEM((2, 2, n_aux * rows, virt), factors.dtype),
+            pltpu.VMEM((width, n_aux * rows), factors.dtype),
+            pltpu.SemaphoreType.DMA((slices, 4)),
+            pltpu.SemaphoreType.DMA((slices, 4)),
             pltpu.SemaphoreType.DMA((slices, planes, 2, 2)),
             pltpu.SemaphoreType.DMA((slices, planes, 2, 2)),
             pltpu.SemaphoreType.DMA((steps, 2, 3)),
             pltpu.SemaphoreType.DMA((steps, 2, 3)),
             pltpu.SemaphoreType.DMA((steps, 2, 4)),
             pltpu.SemaphoreType.DMA((steps, 2, 4)),
+            pltpu.SemaphoreType.DMA((2, 2, n_aux)),
         ],
-        compiler_params=pltpu.CompilerParams(collective_id=0, has_side_effects=True),
-    )(sel)
-
-    half = virt // 2
-    chosen = lax.dynamic_index_in_dim(pair_list, z, 0, keepdims=False)
-    e_i = lax.dynamic_index_in_dim(eps_occ, chosen[0] * orb_local + x, 0, keepdims=False)
-    e_j = lax.dynamic_index_in_dim(eps_occ, chosen[1] * orb_local + y, 0, keepdims=False)
-    contract = (((0,), (0,)), ((), ()))
-    tiles = []
-    for t in range(2):
-        t_col = (t + c) % 2
-        cols = lax.dynamic_slice_in_dim(gath[1], t_col * half, half, 1)
-        tiles.append(
-            lax.dot_general(gath[0, :, t * half : (t + 1) * half], cols, contract, preferred_element_type=jnp.float32)
-        )
-    sums = []
-    for t in range(2):
-        t_col = (t + c) % 2
-        swapped = jnp.where(c == 0, tiles[t], tiles[1 - t]).T
-        rows_e = eps_virt[t * half : (t + 1) * half]
-        cols_e = lax.dynamic_slice_in_dim(eps_virt, t_col * half, half)
-        denominator = rows_e[:, None] + cols_e[None, :] - e_i - e_j
-        sums.append(-jnp.sum(tiles[t] * (2.0 * tiles[t] - swapped) / denominator, axis=1))
-    part = jnp.concatenate(sums)
+        compiler_params=pltpu.CompilerParams(
+            collective_id=0, has_side_effects=True, vmem_limit_bytes=60 * 1024 * 1024
+        ),
+    )(pair_list, near, far, mine)
 
     spread = lax.all_to_all(part.reshape(n_aux, virt // n_aux), "aux", split_axis=0, concat_axis=0, tiled=True)
     every = lax.all_gather(spread, "occ", axis=0, tiled=False)

time: 509 us -> 327 us (0.64)
  local copies, waits for them, and re-layouts: 112 us -> 13.9 us
  waiting for transfers between devices: 46.1 us -> 5.4 us
  matrix products: 40.6 us -> 0 us
  Pallas kernels: 264 us -> 293 us
  between operations: 16.2 us -> 1.42 us
  other arithmetic: 12.3 us -> 2.85 us
    another operation x9 -> x0, local copies, waits for them, and re-layouts: 43.5 us -> none
    all_to_all x1 -> x0, waiting for transfers between devices: 40.7 us -> none  [by_planes(): lax.all_to_all(mine, 'occ', split_axis=2, concat_axis=0, tiled=True)]
    dot_general x2 -> x0, matrix products: 40.6 us -> none  [by_planes(): lax.dot_general(gath[0, :, t * half:(t + 1) * half], cols, contract, pref...]
    pallas_call x1, Pallas kernels: 264 us -> 293 us  [by_planes(): pl.pallas_call(functools.partial(route, planes, slices), out_shape=[jax.S...]
    unnamed x24 -> x2, local copies, waits for them, and re-layouts: 31 us -> 6.7 us
    slice x3 -> x0, local copies, waits for them, and re-layouts: 17.1 us -> none  [the longest x1 16.4 us: by_planes(): cols = lax.dynamic_slice_in_dim(gath[1], t_col * half, half, 1)]
    dot_general x2 -> x0, local copies, waits for them, and re-layouts: 16.3 us -> none  [by_planes(): lax.dot_general(gath[0, :, t * half:(t + 1) * half], cols, contract, pref...]
    reduce_sum x1 -> x0, other arithmetic: 12.2 us -> none  [by_planes(): jnp.sum(tiles[t] * (2.0 * tiles[t] - swapped) / denominator, axis=1)]
  transfers between devices with their start and end apart: 2 -> 1, of which waited for: 2 -> 1; matrix products, arithmetic and copies ran while one was open for 0% -> 0% of each run, Pallas kernels for 0% -> 0%
where the time goes in v2:
time: 327 us
  Pallas kernels  293 us (90%)
  local copies, waits for them, and re-layouts  13.9 us (4%)
  blocking collectives  6.14 us (2%)
  waiting for transfers between devices  5.4 us (2%)
  starting transfers between devices  4.16 us (1%)
    pallas_call x1, Pallas kernels, by_planes(): pl.pallas_call(functools.partial(route, planes, slices), out_shape=[jax.S...  293 us
    unnamed x2, local copies, waits for them, and re-layouts  6.7 us
  transfers between devices with their start and end apart: 1, of which 1 were waited for; matrix products, arithmetic and copies ran while one was open for 0% of the time, Pallas kernels for 0%

profile of v2, /device:TPU:1, one launch (start us, length us, event | category | flops | bytes accessed | tf_op | source)
XLA Modules:
  0.0 326.6 jit_solution(7922999485162149914)
XLA Ops:
  0.0 0.7 constant_dynamic-slice_fusion
  0.8 0.6 fusion
  2.7 1.3 copy.24.pairs
  4.0 0.7 reshape.43
  4.8 0.2 rev.3
  5.0 1.4 fusion.1
  6.4 2.0 subtract_subtract_fusion
  8.4 0.6 sub.43.near
  9.0 1.5 copy.25.far
  10.5 5.4 %copy.30 = bf16[480,2,2560]{2,0,1:T(8,128)(2,1)} copy(bf16[480,2,2560]{2,1,0:T(2,128)(2,1)} %param.4) | data formatting | bytes 9830400 | tf_op args[0]
  15.9 292.7 %shard_map.46 = (f32[2,1,1280]{2,1,0:T(1,128)}, bf16[2,3840,2560]{2,1,0:T(8,128)(2,1)}, bf16[4,2,480,640]{3,2,1,0:T(8,128)(2,1)}) custom-call(s32[4,2]{1,0:T(4,128)} %copy.24.pairs, f32[2,1,1280]{2,1,0:T(1,128)} %sub.43.near, f32[2,1280,1]{2,1,0:T(8,128)} %copy.25.far, bf16[2,480,2560]{2,1,0:T(8,128)(2,1)} %bitcast.13), custom_call_target="tpu_custom_call" | custom-call | tf_op jit(solution)/shard_map/pallas_call | solution.py:296
  308.6 0.7 reduce
  309.3 0.7 all_to_all.8
  310.0 4.2 %all-to-all-start = ((f32[8,1,320]{2,1,0:T(1,128)}), f32[8,1,320]{2,1,0:T(1,128)S(1)}, u32[]{:S(2)}, u32[]{:S(2)}) async-start(f32[8,1,320]{2,1,0:T(1,128)} %all_to_all.8), calls=%async_computation | async-start | bytes 24576 | tf_op jit(solution)/shard_map/all_to_all | solution.py:335
  314.2 5.4 %all-to-all-done = f32[8,1,320]{2,1,0:T(1,128)S(1)} async-done(((f32[8,1,320]{2,1,0:T(1,128)}), f32[8,1,320]{2,1,0:T(1,128)S(1)}, u32[]{:S(2)}, u32[]{:S(2)}) %all-to-all-start) | async-done | bytes 10272 | tf_op jit(solution)/shard_map/all_to_all | solution.py:335
  319.6 6.1 %all-gather = f32[32,1,320]{2,1,0:T(1,128)S(1)} all-gather(f32[8,1,320]{2,1,0:T(1,128)S(1)} %all-to-all-done), channel_id=2, replica_groups=mesh['aux'=8,'occ'=4] {'occ'}, dimensions={0}, use_global_device_ids=true | all-gather | bytes 51200 | tf_op jit(solution)/shard_map/all_gather | solution.py:336
  325.7 0.1 reduce.1
  325.9 0.6 reshape.46
  (5 shorter events, 0.1 us)
Async XLA Ops:
  310.0 9.6 %all-to-all-start = ((f32[8,1,320]{2,1,0:T(1,128)}), f32[8,1,320]{2,1,0:T(1,128)S(1)}, u32[]{:S(2)}, u32[]{:S(2)}) async-start(f32[8,1,320]{2,1,0:T(1,128)} %all_to_all.8), calls=%async_computation | async-start | bytes 24576 | tf_op jit(solution)/shard_map/all_to_all | solution.py:335

commit v3 on v2

--- a/solution.py
+++ b/solution.py
@@ -15,8 +15,8 @@
 
 
 def route(
-    planes, slices, pairs, near, far, mine, part, gath, zbuf, quarter, sel, acc, held, turned,
-    o_send, o_recv, z_send, z_recv, hop_send, hop_recv, core_send, core_recv, held_sem,
+    planes, slices, pairs, e_occ, e_virt, mine, every, gath, zbuf, quarter, sel, acc, rec, held, turned, part,
+    fin_send, fin_recv, o_send, o_recv, z_send, z_recv, hop_send, hop_recv, core_send, core_recv, held_sem,
 ):
     depth, virt = mine.shape[1], mine.shape[2]
     rows = depth // slices
@@ -33,12 +33,24 @@
     def fellow(d):
         return {"aux": aux, "occ": flip(occ, d)}
 
+    def source(m):
+        return device(occ, m // 4, m // 2 % 2, m % 2)
+
+    def is_me(m):
+        return (occ == z) & (m == x * 4 + y * 2 + c)
+
     partners = [device(flip(z, k), x, y, c) for k in range(1, planes)]
     partners += [fellow(d) for d in range(1, 4)] + [device(z, 1 - x, y, c)]
     barrier = pltpu.get_barrier_semaphore()
     for partner in partners:
         pl.semaphore_signal(barrier, inc=1, device_id=partner, device_id_type=MESH)
-    pl.semaphore_wait(barrier, len(partners))
+    for m in range(8):
+
+        @pl.when(jnp.logical_not(is_me(m)))
+        def _():
+            pl.semaphore_signal(barrier, inc=1, device_id=source(m), device_id_type=MESH)
+
+    pl.semaphore_wait(barrier, len(partners) + 8 - jnp.where(z == occ, 1, 0))
 
     def span(t):
         return pl.ds(pl.multiple_of(t * rows, 16), rows)
@@ -140,8 +152,6 @@
                 o_copy(t, d).wait()
             else:
                 o_copy(t, d).wait_recv()
-        if t + 2 < slices:
-            start_exchange(t + 2)
         for p in range(planes):
             for s in range(2):
                 block = pairs[p, s]
@@ -153,22 +163,64 @@
                 for k in (2, 3, 1):
                     z_copy(t, k, s, rel).start()
 
-    start_exchange(0)
-    if slices > 1:
-        start_exchange(1)
+    def last(a):
+        return pltpu.make_async_remote_copy(
+            src_ref=part,
+            dst_ref=every.at[x * 4 + y * 2 + c],
+            send_sem=fin_send.at[a],
+            recv_sem=fin_recv.at[x * 4 + y * 2 + c],
+            device_id={"aux": a, "occ": z},
+            device_id_type=MESH,
+        )
+
+    def last_keep():
+        m = x * 4 + y * 2 + c
+        return pltpu.make_async_copy(part, every.at[m], fin_recv.at[m])
+
+    def last_from(m):
+        return pltpu.make_async_remote_copy(
+            src_ref=part,
+            dst_ref=every.at[m],
+            send_sem=fin_send.at[m],
+            recv_sem=fin_recv.at[m],
+            device_id=source(m),
+            device_id_type=MESH,
+        )
+
+    for t in range(min(2, slices)):
+        start_exchange(t)
+
+    e_i = e_occ[pairs[z, 0] * 2 + x]
+    e_j = e_occ[pairs[z, 1] * 2 + y]
 
     @pl.loop(0, 2 * (half // 128))
     def _(r):
         tile, blk = r // (half // 128), r % (half // 128)
         acc[tile, pl.ds(pl.multiple_of(blk * 128, 128), 128), :] = jnp.zeros((128, half), jnp.float32)
 
+    @pl.loop(0, 2 * (half // 128))
+    def _(r):
+        tile, blk = r // (half // 128), r % (half // 128)
+        at = pl.ds(pl.multiple_of(blk * 128, 128), 128)
+        first = pl.multiple_of((tile + c) % 2 * half + blk * 128, 128)
+        far = jnp.broadcast_to(e_virt[:, pl.ds(first, 128)], (128, 128)).T
+        for g in range(half // 128):
+            near = e_virt[:, pl.ds(pl.multiple_of(tile * half + g * 128, 128), 128)]
+            rec[tile, at, g * 128 : (g + 1) * 128] = 1.0 / (near + far - e_i - e_j)
+
     choose(0)
+    for t in range(2, min(4, slices)):
+        start_exchange(t)
+    if slices > 1:
+        choose(1)
+    for t in range(4, slices):
+        start_exchange(t)
 
     @pl.loop(0, steps + 8)
     def _(n):
-        for t in range(1, slices):
-
-            @pl.when(n == max(0, planes * t - 6))
+        for t in range(2, slices):
+
+            @pl.when(n == planes * (t - 2))
             def _():
                 choose(t)
 
@@ -248,9 +300,21 @@
         at = pl.ds(pl.multiple_of(blk * 128, 128), 128)
         direct = acc[tile, at, :].T
         swapped = acc[(tile + c) % 2, :, at]
-        denominator = far[tile] + near[tile, :, at]
-        value = direct * (2.0 * direct - swapped) / denominator
+        value = direct * (2.0 * direct - swapped) * rec[tile, :, at]
         part[tile, :, at] = -jnp.sum(value, axis=0, keepdims=True)
+
+    def to_me(a):
+        return (z == occ) & (a == aux)
+
+    for a in range(8):
+
+        @pl.when(to_me(a))
+        def _():
+            last_keep().start()
+
+        @pl.when(jnp.logical_not(to_me(a)))
+        def _():
+            last(a).start()
 
     for t in range(slices):
         for d in (1, 2, 3):
@@ -270,6 +334,22 @@
                 hop(n, s, kind).wait_send()
             for kind in range(4):
                 across(n, s, kind).wait_send()
+
+    for m in range(8):
+
+        @pl.when(is_me(m))
+        def _():
+            last_keep().wait()
+
+        @pl.when(jnp.logical_not(is_me(m)))
+        def _():
+            last_from(m).wait_recv()
+
+    for a in range(8):
+
+        @pl.when(jnp.logical_not(to_me(a)))
+        def _():
+            last(a).wait_send()
 
 
 def by_planes(factors, pair_list, eps_occ, eps_virt):
@@ -282,27 +362,18 @@
     rows = local_q // slices
     steps = planes * slices
     aux = lax.axis_index("aux")
-    occ = lax.axis_index("occ")
-    z, x, y, c = aux // 2, aux % 2, occ // 2, occ % 2
-
-    chosen = lax.dynamic_index_in_dim(pair_list, z, 0, keepdims=False)
-    e_i = lax.dynamic_index_in_dim(eps_occ, chosen[0] * orb_local + x, 0, keepdims=False)
-    e_j = lax.dynamic_index_in_dim(eps_occ, chosen[1] * orb_local + y, 0, keepdims=False)
-    halves = eps_virt.reshape(2, half)
-    near = (halves - e_i - e_j).reshape(2, 1, half)
-    far = jnp.where(c == 0, halves, halves[::-1]).reshape(2, half, 1)
     mine = factors.transpose(1, 0, 2)
 
-    part, _, _ = pl.pallas_call(
+    every, _, _ = pl.pallas_call(
         functools.partial(route, planes, slices),
         out_shape=[
-            jax.ShapeDtypeStruct((2, 1, half), jnp.float32),
+            jax.ShapeDtypeStruct((8, 2, 1, half), jnp.float32),
             jax.ShapeDtypeStruct((2, n_aux * local_q, virt), factors.dtype),
             jax.ShapeDtypeStruct((planes, 2, local_q, width), factors.dtype),
         ],
         in_specs=[
             pl.BlockSpec(memory_space=pltpu.SMEM),
-            pl.BlockSpec(memory_space=pltpu.VMEM),
+            pl.BlockSpec(memory_space=pltpu.SMEM),
             pl.BlockSpec(memory_space=pltpu.VMEM),
             pl.BlockSpec(memory_space=pl.ANY),
         ],
@@ -315,8 +386,12 @@
             [pltpu.VMEM((4, 2, rows, width), factors.dtype) for _ in range(slices)],
             pltpu.VMEM((slices, planes, 2, 2, rows, width), factors.dtype),
             pltpu.VMEM((2, half, half), jnp.float32),
+            pltpu.VMEM((2, half, half), jnp.float32),
             pltpu.VMEM((2, 2, n_aux * rows, virt), factors.dtype),
             pltpu.VMEM((width, n_aux * rows), factors.dtype),
+            pltpu.VMEM((2, 1, half), jnp.float32),
+            pltpu.SemaphoreType.DMA((8,)),
+            pltpu.SemaphoreType.DMA((8,)),
             pltpu.SemaphoreType.DMA((slices, 4)),
             pltpu.SemaphoreType.DMA((slices, 4)),
             pltpu.SemaphoreType.DMA((slices, planes, 2, 2)),
@@ -330,13 +405,10 @@
         compiler_params=pltpu.CompilerParams(
             collective_id=0, has_side_effects=True, vmem_limit_bytes=60 * 1024 * 1024
         ),
-    )(pair_list, near, far, mine)
-
-    spread = lax.all_to_all(part.reshape(n_aux, virt // n_aux), "aux", split_axis=0, concat_axis=0, tiled=True)
-    every = lax.all_gather(spread, "occ", axis=0, tiled=False)
-    every = every.reshape(2, 2, planes, 2, virt // n_aux).sum(axis=1)
-    own = lax.dynamic_index_in_dim(every, occ, 1, keepdims=False)
-    return own.transpose(1, 0, 2).reshape(1, 4, virt // n_aux)
+    )(pair_list, eps_occ, eps_virt.reshape(1, virt), mine)
+
+    totals = every.reshape(4, 2, virt).sum(axis=1)
+    return lax.dynamic_slice_in_dim(totals, aux * (virt // n_aux), virt // n_aux, 1)[None]
 
 
 def by_groups(factors, pair_list, eps_occ, eps_virt):

time: 327 us -> 315 us (0.963); the launches traced: 327 us -> 311 us
  Pallas kernels: 293 us -> 301 us
  blocking collectives: 6.14 us -> 0 us
  waiting for transfers between devices: 5.4 us -> 0 us
  local copies, waits for them, and re-layouts: 13.9 us -> 8.76 us
  starting transfers between devices: 4.16 us -> 0 us
    pallas_call x1, Pallas kernels: 293 us -> 301 us  [by_planes(): pl.pallas_call(functools.partial(route, planes, slices), out_shape=[jax.S...]
    all_gather x1 -> x0, blocking collectives: 6.14 us -> none  [by_planes(): every = lax.all_gather(spread, 'occ', axis=0, tiled=False)]
    all_to_all x1 -> x0, waiting for transfers between devices: 5.4 us -> none  [by_planes(): lax.all_to_all(part.reshape(n_aux, virt // n_aux), 'aux', split_axis=0, c...]
    all_to_all x1 -> x0, starting transfers between devices: 4.16 us -> none  [by_planes(): lax.all_to_all(part.reshape(n_aux, virt // n_aux), 'aux', split_axis=0, c...]
  transfers between devices with their start and end apart: 1 -> 0, of which waited for: 1 -> 0; matrix products, arithmetic and copies ran while one was open for 0% -> 0% of each run, Pallas kernels for 0% -> 0%
where the time goes in v3:
time: 315 us; the launch traced here: 311 us
  Pallas kernels  301 us (96%)
  local copies, waits for them, and re-layouts  8.76 us (3%)
    pallas_call x1, Pallas kernels, by_planes(): pl.pallas_call(functools.partial(route, planes, slices), out_shape=[jax.S...  301 us
    unnamed x2, local copies, waits for them, and re-layouts  6.69 us

profile of v3, /device:TPU:1, one launch (start us, length us, event | category | flops | bytes accessed | tf_op | source)
XLA Modules:
  0.0 311.0 jit_solution(14187242469540845431)
XLA Ops:
  0.0 1.3 copy.6.pairs
  1.3 1.3 reshape.6.e_virt
  2.6 5.4 %copy.8 = bf16[480,2,2560]{2,0,1:T(8,128)(2,1)} copy(bf16[480,2,2560]{2,1,0:T(2,128)(2,1)} %param.4) | data formatting | bytes 9830400 | tf_op args[0]
  8.0 300.9 %shard_map.46 = (f32[8,2,1,1280]{3,2,1,0:T(1,128)}, bf16[2,3840,2560]{2,1,0:T(8,128)(2,1)}, bf16[4,2,480,640]{3,2,1,0:T(8,128)(2,1)}) custom-call(s32[4,2]{1,0:T(4,128)} %copy.6.pairs, f32[8]{0:T(128)} %e_occ.1, f32[1,2560]{1,0:T(1,128)} %reshape.6.e_virt, bf16[2,480,2560]{2,1,0:T(8,128)(2,1)} %bitcast.5), custom_call_target="tpu_custom_call" | custom-call | tf_op jit(solution)/shard_map/pallas_call | solution.py:367
  309.0 1.1 reduce
  310.1 0.1 reshape.7
  310.2 0.1 reduce_sum.9
  310.3 0.7 dynamic-slice_bitcast_fusion

commit v4 on v3

--- a/solution.py
+++ b/solution.py
@@ -22,7 +22,7 @@
     rows = depth // slices
     width = virt // 4
     half = virt // 2
-    steps = planes * slices
+    steps = 2 * planes * slices
     aux = lax.axis_index("aux")
     occ = lax.axis_index("occ")
     z, x, y, c = aux // 2, aux % 2, occ // 2, occ % 2
@@ -56,13 +56,13 @@
         return pl.ds(pl.multiple_of(t * rows, 16), rows)
 
     def place(s, zs, xs, ys, cs, t):
-        first = pl.multiple_of((zs * 2 + xs) * depth + t * rows, 16)
-        left = pl.multiple_of((ys * 2 + cs) * width, 128)
-        return gath.at[s, pl.ds(first, rows), pl.ds(left, width)]
+        left = pl.multiple_of((cs * 2 + ys) * width, 128)
+        return gath.at[s, zs, xs, span(t), pl.ds(left, width)]
 
     def o_copy(t, d):
         to = flip(occ, d)
-        src = mine.at[:, pl.ds(t * rows, rows), pl.ds(pl.multiple_of(to * width, 128), width)]
+        left = pl.multiple_of((to % 2 * 2 + to // 2) * width, 128)
+        src = mine.at[:, pl.ds(t * rows, rows), pl.ds(left, width)]
         if d == 0:
             return pltpu.make_async_copy(src, quarter[t].at[occ], o_recv.at[t, 0])
         return pltpu.make_async_remote_copy(
@@ -76,7 +76,7 @@
 
     def z_copy(t, k, s, rel):
         zt = flip(z, k)
-        own = x if s == 0 else y
+        own = x * (1 - s) + y * s
         w = own if rel == 0 else 1 - own
         dst = place(s, z, x, y, c, t) if rel == 0 else zbuf.at[k, s, span(t), :]
         return pltpu.make_async_remote_copy(
@@ -89,58 +89,52 @@
         )
 
     def z_keep(t, s, rel):
-        own = x if s == 0 else y
+        own = x * (1 - s) + y * s
         w = own if rel == 0 else 1 - own
         dst = place(s, z, x, y, c, t) if rel == 0 else zbuf.at[0, s, span(t), :]
         return pltpu.make_async_copy(sel.at[t, z, s, w], dst, z_recv.at[t, 0, s, rel])
 
-    def hop(n, s, kind):
-        t, k = n // planes, n % planes
+    def parts_of(n):
+        j = n % planes
+        return n // (2 * planes), n // planes % 2, jnp.minimum(j, 1) * (1 + j % 3)
+
+    def hop(n, kind):
+        t, s, k = parts_of(n)
         zs = flip(z, k)
-        share = device(z, x, 1 - y, c) if s == 0 else device(z, 1 - x, y, c)
-        other = device(z, 1 - x, y, c) if s == 0 else device(z, x, 1 - y, c)
-        xs, ys = (1 - x, y) if s == 0 else (x, 1 - y)
+        xf, yf = x + s * (1 - 2 * x), y + (1 - s) * (1 - 2 * y)
+        xo, yo = x + (1 - s) * (1 - 2 * x), y + s * (1 - 2 * y)
+        share, other = device(z, xf, yf, c), device(z, xo, yo, c)
         own = place(s, zs, x, y, c, t)
         if kind == 0:
             src, dst, target = own, own, share
         elif kind == 1:
             src, dst, target = zbuf.at[k, s, span(t), :], own, other
         else:
-            src = place(s, zs, xs, ys, c, t)
+            src = place(s, zs, xo, yo, c, t)
             dst, target = src, share
         return pltpu.make_async_remote_copy(
             src_ref=src,
             dst_ref=dst,
-            send_sem=hop_send.at[n, s, kind],
-            recv_sem=hop_recv.at[n, s, kind],
+            send_sem=hop_send.at[n, kind],
+            recv_sem=hop_recv.at[n, kind],
             device_id=target,
             device_id_type=MESH,
         )
 
-    def across(n, s, kind):
-        t, k = n // planes, n % planes
-        zs = flip(z, k)
-        if s == 0:
-            spots = [(x, y), (x, 1 - y), (1 - x, y), (1 - x, 1 - y)]
-        else:
-            spots = [(x, y), (1 - x, y), (x, 1 - y), (1 - x, 1 - y)]
-        ref = place(s, zs, spots[kind][0], spots[kind][1], c, t)
+    def across(n):
+        t, s, k = parts_of(n)
+        ref = gath.at[s, flip(z, k), :, span(t), pl.ds(pl.multiple_of(c * half, 128), half)]
         return pltpu.make_async_remote_copy(
             src_ref=ref,
             dst_ref=ref,
-            send_sem=core_send.at[n, s, kind],
-            recv_sem=core_recv.at[n, s, kind],
+            send_sem=core_send.at[n],
+            recv_sem=core_recv.at[n],
             device_id=device(z, x, y, 1 - c),
             device_id_type=MESH,
         )
 
-    def fetch(t, s, q):
-        first = pl.multiple_of(q * depth + t * rows, 16)
-        return pltpu.make_async_copy(
-            gath.at[s, pl.ds(first, rows), :],
-            held.at[t % 2, s, pl.ds(q * rows, rows), :],
-            held_sem.at[t % 2, s, q],
-        )
+    def fetch(t, s):
+        return pltpu.make_async_copy(gath.at[s, :, :, span(t), :], held.at[t % 2, s], held_sem.at[t % 2, s])
 
     def start_exchange(t):
         for d in (2, 3, 1, 0):
@@ -160,7 +154,8 @@
         for s in range(2):
             for rel in (1, 0):
                 z_keep(t, s, rel).start()
-                for k in (2, 3, 1):
+            for k in (2, 3, 1):
+                for rel in (1, 0):
                     z_copy(t, k, s, rel).start()
 
     def last(a):
@@ -192,6 +187,10 @@
 
     e_i = e_occ[pairs[z, 0] * 2 + x]
     e_j = e_occ[pairs[z, 1] * 2 + y]
+
+    choose(0)
+    for t in range(2, min(4, slices)):
+        start_exchange(t)
 
     @pl.loop(0, 2 * (half // 128))
     def _(r):
@@ -208,90 +207,79 @@
             near = e_virt[:, pl.ds(pl.multiple_of(tile * half + g * 128, 128), 128)]
             rec[tile, at, g * 128 : (g + 1) * 128] = 1.0 / (near + far - e_i - e_j)
 
-    choose(0)
-    for t in range(2, min(4, slices)):
-        start_exchange(t)
     if slices > 1:
         choose(1)
-    for t in range(4, slices):
+    for t in range(4, min(6, slices)):
         start_exchange(t)
 
-    @pl.loop(0, steps + 8)
+    @pl.loop(0, steps + 12)
     def _(n):
         for t in range(2, slices):
 
-            @pl.when(n == planes * (t - 2))
+            @pl.when(n == 2 * planes * (t - 2))
             def _():
                 choose(t)
+                if t + 4 < slices:
+                    start_exchange(t + 4)
 
         @pl.when(n < steps)
         def _():
-            t, k = n // planes, n % planes
+            t, s, k = parts_of(n)
+            for rel in (1, 0):
+
+                @pl.when(k == 0)
+                def _():
+                    z_keep(t, s, rel).wait()
+
+                @pl.when(k > 0)
+                def _():
+                    z_copy(t, k, s, rel).wait_recv()
+
+                hop(n, rel).start()
+
+        @pl.when((n >= 1) & (n < steps + 1))
+        def _():
+            hop(n - 1, 1).wait_recv()
+            hop(n - 1, 2).start()
+
+        @pl.when((n >= 2) & (n < steps + 2))
+        def _():
+            hop(n - 2, 0).wait_recv()
+            hop(n - 2, 2).wait_recv()
+            across(n - 2).start()
+
+        @pl.when((n >= 3) & (n < steps + 3))
+        def _():
+            across(n - 3).wait_recv()
+
+        @pl.when((n >= 10) & (n < steps + 10) & (n % 8 == 2))
+        def _():
             for s in range(2):
-                for rel in (1, 0):
-
-                    @pl.when(k == 0)
-                    def _():
-                        z_keep(t, s, rel).wait()
-
-                    @pl.when(k > 0)
-                    def _():
-                        z_copy(t, k, s, rel).wait_recv()
-
-                    hop(n, s, rel).start()
-                    if rel == 0:
-                        across(n, s, 0).start()
-
-        @pl.when((n >= 1) & (n < steps + 1))
-        def _():
-            for s in range(2):
-                hop(n - 1, s, 1).wait_recv()
-                hop(n - 1, s, 2).start()
-                across(n - 1, s, 2).start()
-
-        @pl.when((n >= 2) & (n < steps + 2))
-        def _():
-            for s in range(2):
-                hop(n - 2, s, 0).wait_recv()
-                across(n - 2, s, 1).start()
-                hop(n - 2, s, 2).wait_recv()
-                across(n - 2, s, 3).start()
-
-        @pl.when((n >= 3) & (n < steps + 3))
-        def _():
-            for s in range(2):
-                for kind in range(4):
-                    across(n - 3, s, kind).wait_recv()
-
-        @pl.when((n >= 6) & (n < steps + 6) & (n % planes == 2))
-        def _():
-            t = (n - 6) // planes
-            for s in range(2):
-                for q in range(2 * planes):
-                    fetch(t, s, q).start()
-
-        @pl.when(n >= 8)
-        def _():
-            t, unit = (n - 8) // planes, n % planes
+                fetch((n - 10) // 8, s).start()
+
+        @pl.when((n >= 12) & (n % 2 == 0))
+        def _():
+            t, unit = (n - 12) // 8, (n - 12) % 8 // 2
 
             @pl.when(unit == 0)
             def _():
                 for s in range(2):
-                    for q in range(2 * planes):
-                        fetch(t, s, q).wait()
+                    fetch(t, s).wait()
 
             tile = unit // 2
             top = pl.multiple_of(unit % 2 * width, 128)
             left = pl.multiple_of((tile + c) % 2 * half, 128)
             lhs = pl.multiple_of(tile * half + unit % 2 * width, 128)
-            turned[...] = held[t % 2, 0, :, pl.ds(lhs, width)].T
+            turned[...] = held[t % 2, 0, :, :, :, pl.ds(lhs, width)].reshape(2 * planes * rows, width).T
 
             @pl.loop(0, half // 256)
             def _(col):
                 cols = pl.ds(pl.multiple_of(left + col * 256, 128), 256)
                 into = pl.ds(pl.multiple_of(col * 256, 128), 256)
                 acc[tile, pl.ds(top, width), into] += jnp.dot(
-                    turned[...], held[t % 2, 1, :, cols], preferred_element_type=jnp.float32
+                    turned[...],
+                    held[t % 2, 1, :, :, :, cols].reshape(2 * planes * rows, 256),
+                    preferred_element_type=jnp.float32,
                 )
 
     @pl.loop(0, 2 * (half // 128))
@@ -329,11 +317,9 @@
 
     @pl.loop(0, steps)
     def _(n):
-        for s in range(2):
-            for kind in range(3):
-                hop(n, s, kind).wait_send()
-            for kind in range(4):
-                across(n, s, kind).wait_send()
+        for kind in range(3):
+            hop(n, kind).wait_send()
+        across(n).wait_send()
 
     for m in range(8):
 
@@ -358,9 +344,9 @@
     planes = pair_list.shape[0]
     width = virt // 4
     half = virt // 2
-    slices = next(n for n in (5, 3, 2, 1) if local_q % (16 * n) == 0)
+    slices = next(n for n in (10, 5, 3, 2, 1) if local_q % (16 * n) == 0)
     rows = local_q // slices
-    steps = planes * slices
+    steps = 2 * planes * slices
     aux = lax.axis_index("aux")
     mine = factors.transpose(1, 0, 2)
 
@@ -368,7 +354,7 @@
         functools.partial(route, planes, slices),
         out_shape=[
             jax.ShapeDtypeStruct((8, 2, 1, half), jnp.float32),
-            jax.ShapeDtypeStruct((2, n_aux * local_q, virt), factors.dtype),
+            jax.ShapeDtypeStruct((2, planes, 2, local_q, virt), factors.dtype),
             jax.ShapeDtypeStruct((planes, 2, local_q, width), factors.dtype),
         ],
         in_specs=[
@@ -387,7 +373,7 @@
             pltpu.VMEM((slices, planes, 2, 2, rows, width), factors.dtype),
             pltpu.VMEM((2, half, half), jnp.float32),
             pltpu.VMEM((2, half, half), jnp.float32),
-            pltpu.VMEM((2, 2, n_aux * rows, virt), factors.dtype),
+            pltpu.VMEM((2, 2, planes, 2, rows, virt), factors.dtype),
             pltpu.VMEM((width, n_aux * rows), factors.dtype),
             pltpu.VMEM((2, 1, half), jnp.float32),
             pltpu.SemaphoreType.DMA((8,)),
@@ -396,11 +382,11 @@
             pltpu.SemaphoreType.DMA((slices, 4)),
             pltpu.SemaphoreType.DMA((slices, planes, 2, 2)),
             pltpu.SemaphoreType.DMA((slices, planes, 2, 2)),
-            pltpu.SemaphoreType.DMA((steps, 2, 3)),
-            pltpu.SemaphoreType.DMA((steps, 2, 3)),
-            pltpu.SemaphoreType.DMA((steps, 2, 4)),
-            pltpu.SemaphoreType.DMA((steps, 2, 4)),
-            pltpu.SemaphoreType.DMA((2, 2, n_aux)),
+            pltpu.SemaphoreType.DMA((steps, 3)),
+            pltpu.SemaphoreType.DMA((steps, 3)),
+            pltpu.SemaphoreType.DMA((steps,)),
+            pltpu.SemaphoreType.DMA((steps,)),
+            pltpu.SemaphoreType.DMA((2, 2)),
         ],
         compiler_params=pltpu.CompilerParams(
             collective_id=0, has_side_effects=True, vmem_limit_bytes=60 * 1024 * 1024

time: 315 us -> 358 us (1.14)
  Pallas kernels: 301 us -> 347 us
    pallas_call x1, Pallas kernels: 301 us -> 347 us  [by_planes(): pl.pallas_call(functools.partial(route, planes, slices), out_shape=[jax.S...]
where the time goes in v4:
time: 358 us; the launch traced here: 357 us
  Pallas kernels  347 us (97%)
  local copies, waits for them, and re-layouts  8.76 us (2%)
    pallas_call x1, Pallas kernels, by_planes(): pl.pallas_call(functools.partial(route, planes, slices), out_shape=[jax.S...  347 us

profile of v4, /device:TPU:1, one launch (start us, length us, event | category | flops | bytes accessed | tf_op | source)
XLA Modules:
  0.0 357.0 jit_solution(11161312044474828559)
XLA Ops:
  0.0 1.3 copy.6.pairs
  1.3 1.3 reshape.6.e_virt
  2.6 5.4 %copy.8 = bf16[480,2,2560]{2,0,1:T(8,128)(2,1)} copy(bf16[480,2,2560]{2,1,0:T(2,128)(2,1)} %param.4) | data formatting | bytes 9830400 | tf_op args[0]
  8.0 347.0 %shard_map.46 = (f32[8,2,1,1280]{3,2,1,0:T(1,128)}, bf16[2,4,2,480,2560]{4,3,2,1,0:T(8,128)(2,1)}, bf16[4,2,480,640]{3,2,1,0:T(8,128)(2,1)}) custom-call(s32[4,2]{1,0:T(4,128)} %copy.6.pairs, f32[8]{0:T(128)} %e_occ.1, f32[1,2560]{1,0:T(1,128)} %reshape.6.e_virt, bf16[2,480,2560]{2,1,0:T(8,128)(2,1)} %bitcast.5), custom_call_target="tpu_custom_call" | custom-call | tf_op jit(solution)/shard_map/pallas_call | solution.py:353
  355.0 1.1 reduce
  356.1 0.1 reshape.7
  356.2 0.1 reduce_sum.9
  356.3 0.7 dynamic-slice_bitcast_fusion

commit v5 on v4

--- a/solution.py
+++ b/solution.py
@@ -22,6 +22,8 @@
     rows = depth // slices
     width = virt // 4
     half = virt // 2
+    lag = 3
+    ready = 3 * lag + 7
     steps = 2 * planes * slices
     aux = lax.axis_index("aux")
     occ = lax.axis_index("occ")
@@ -212,7 +214,7 @@
     for t in range(4, min(6, slices)):
         start_exchange(t)
 
-    @pl.loop(0, steps + 12)
+    @pl.loop(0, steps + ready + 1)
     def _(n):
         for t in range(2, slices):
 
@@ -237,29 +239,29 @@
 
                 hop(n, rel).start()
 
-        @pl.when((n >= 1) & (n < steps + 1))
-        def _():
-            hop(n - 1, 1).wait_recv()
-            hop(n - 1, 2).start()
-
-        @pl.when((n >= 2) & (n < steps + 2))
-        def _():
-            hop(n - 2, 0).wait_recv()
-            hop(n - 2, 2).wait_recv()
-            across(n - 2).start()
-
-        @pl.when((n >= 3) & (n < steps + 3))
-        def _():
-            across(n - 3).wait_recv()
-
-        @pl.when((n >= 10) & (n < steps + 10) & (n % 8 == 2))
+        @pl.when((n >= lag) & (n < steps + lag))
+        def _():
+            hop(n - lag, 1).wait_recv()
+            hop(n - lag, 2).start()
+
+        @pl.when((n >= 2 * lag) & (n < steps + 2 * lag))
+        def _():
+            hop(n - 2 * lag, 0).wait_recv()
+            hop(n - 2 * lag, 2).wait_recv()
+            across(n - 2 * lag).start()
+
+        @pl.when((n >= 3 * lag) & (n < steps + 3 * lag))
+        def _():
+            across(n - 3 * lag).wait_recv()
+
+        @pl.when((n >= ready) & (n < steps + ready) & ((n - ready) % 8 == 0))
         def _():
             for s in range(2):
-                fetch((n - 10) // 8, s).start()
-
-        @pl.when((n >= 12) & (n % 2 == 0))
-        def _():
-            t, unit = (n - 12) // 8, (n - 12) % 8 // 2
+                fetch((n - ready) // 8, s).start()
+
+        @pl.when((n >= ready + 2) & ((n - ready) % 2 == 0))
+        def _():
+            t, unit = (n - ready - 2) // 8, (n - ready - 2) % 8 // 2
 
             @pl.when(unit == 0)
             def _():
@@ -344,7 +346,7 @@
     planes = pair_list.shape[0]
     width = virt // 4
     half = virt // 2
-    slices = next(n for n in (10, 5, 3, 2, 1) if local_q % (16 * n) == 0)
+    slices = next(n for n in (5, 3, 2, 1) if local_q % (16 * n) == 0)
     rows = local_q // slices
     steps = 2 * planes * slices
     aux = lax.axis_index("aux")

time: 358 us -> 317 us (0.89)
  Pallas kernels: 347 us -> 307 us
    pallas_call x1, Pallas kernels: 347 us -> 307 us  [by_planes(): pl.pallas_call(functools.partial(route, planes, slices), out_shape=[jax.S...]
where the time goes in v5:
time: 317 us
  Pallas kernels  307 us (97%)
  local copies, waits for them, and re-layouts  8.76 us (3%)
    pallas_call x1, Pallas kernels, by_planes(): pl.pallas_call(functools.partial(route, planes, slices), out_shape=[jax.S...  307 us
    unnamed x2, local copies, waits for them, and re-layouts  6.69 us

profile of v5, /device:TPU:1, one launch (start us, length us, event | category | flops | bytes accessed | tf_op | source)
XLA Modules:
  0.0 316.6 jit_solution(8838887331304792496)
XLA Ops:
  0.0 1.3 copy.6.pairs
  1.3 1.3 reshape.6.e_virt
  2.6 5.4 %copy.8 = bf16[480,2,2560]{2,0,1:T(8,128)(2,1)} copy(bf16[480,2,2560]{2,1,0:T(2,128)(2,1)} %param.4) | data formatting | bytes 9830400 | tf_op args[0]
  8.0 306.6 %shard_map.46 = (f32[8,2,1,1280]{3,2,1,0:T(1,128)}, bf16[2,4,2,480,2560]{4,3,2,1,0:T(8,128)(2,1)}, bf16[4,2,480,640]{3,2,1,0:T(8,128)(2,1)}) custom-call(s32[4,2]{1,0:T(4,128)} %copy.6.pairs, f32[8]{0:T(128)} %e_occ.1, f32[1,2560]{1,0:T(1,128)} %reshape.6.e_virt, bf16[2,480,2560]{2,1,0:T(8,128)(2,1)} %bitcast.5), custom_call_target="tpu_custom_call" | custom-call | tf_op jit(solution)/shard_map/pallas_call | solution.py:355
  314.6 1.1 reduce
  315.7 0.1 reshape.7
  315.9 0.1 reduce_sum.9
  316.0 0.7 dynamic-slice_bitcast_fusion

commit v6 on v5

--- a/solution.py
+++ b/solution.py
@@ -29,6 +29,8 @@
     occ = lax.axis_index("occ")
     z, x, y, c = aux // 2, aux % 2, occ // 2, occ % 2
 
+    inner = (z + 1) // 2 % 2
+
     def device(z_, x_, y_, c_):
         return {"aux": z_ * 2 + x_, "occ": y_ * 2 + c_}
 
@@ -98,7 +100,8 @@
 
     def parts_of(n):
         j = n % planes
-        return n // (2 * planes), n // planes % 2, jnp.minimum(j, 1) * (1 + j % 3)
+        k = j + inner * (j % 2 * (1 - j // 2) - (1 - j % 2) * (j // 2))
+        return n // (2 * planes), n // planes % 2, k
 
     def hop(n, kind):
         t, s, k = parts_of(n)
@@ -156,7 +159,7 @@
         for s in range(2):
             for rel in (1, 0):
                 z_keep(t, s, rel).start()
-            for k in (2, 3, 1):
+            for k in (2 - inner, 1 + inner, 3):
                 for rel in (1, 0):
                     z_copy(t, k, s, rel).start()
 

time: 317 us -> 310 us (0.978)
  Pallas kernels: 307 us -> 300 us
    pallas_call x1, Pallas kernels: 307 us -> 300 us  [by_planes(): pl.pallas_call(functools.partial(route, planes, slices), out_shape=[jax.S...]
where the time goes in v6:
time: 310 us
  Pallas kernels  300 us (97%)
  local copies, waits for them, and re-layouts  8.76 us (3%)
    pallas_call x1, Pallas kernels, by_planes(): pl.pallas_call(functools.partial(route, planes, slices), out_shape=[jax.S...  300 us
    unnamed x2, local copies, waits for them, and re-layouts  6.69 us

profile of v6, /device:TPU:1, one launch (start us, length us, event | category | flops | bytes accessed | tf_op | source)
XLA Modules:
  0.0 309.7 jit_solution(7662406728487503812)
XLA Ops:
  0.0 1.3 copy.6.pairs
  1.3 1.3 reshape.6.e_virt
  2.6 5.4 %copy.8 = bf16[480,2,2560]{2,0,1:T(8,128)(2,1)} copy(bf16[480,2,2560]{2,1,0:T(2,128)(2,1)} %param.4) | data formatting | bytes 9830400 | tf_op args[0]
  8.0 299.7 %shard_map.46 = (f32[8,2,1,1280]{3,2,1,0:T(1,128)}, bf16[2,4,2,480,2560]{4,3,2,1,0:T(8,128)(2,1)}, bf16[4,2,480,640]{3,2,1,0:T(8,128)(2,1)}) custom-call(s32[4,2]{1,0:T(4,128)} %copy.6.pairs, f32[8]{0:T(128)} %e_occ.1, f32[1,2560]{1,0:T(1,128)} %reshape.6.e_virt, bf16[2,480,2560]{2,1,0:T(8,128)(2,1)} %bitcast.5), custom_call_target="tpu_custom_call" | custom-call | tf_op jit(solution)/shard_map/pallas_call | solution.py:358
  307.7 1.1 reduce
  308.8 0.1 reshape.7
  308.9 0.1 reduce_sum.9
  309.1 0.7 dynamic-slice_bitcast_fusion

commit v7 on v6

--- a/solution.py
+++ b/solution.py
@@ -22,7 +22,7 @@
     rows = depth // slices
     width = virt // 4
     half = virt // 2
-    lag = 3
+    lag = 2
     ready = 3 * lag + 7
     steps = 2 * planes * slices
     aux = lax.axis_index("aux")
@@ -139,7 +139,7 @@
         )
 
     def fetch(t, s):
-        return pltpu.make_async_copy(gath.at[s, :, :, span(t), :], held.at[t % 2, s], held_sem.at[t % 2, s])
+        return pltpu.make_async_copy(gath.at[s, :, :, span(t), :], held.at[s], held_sem.at[s])
 
     def start_exchange(t):
         for d in (2, 3, 1, 0):
@@ -187,14 +187,13 @@
             device_id_type=MESH,
         )
 
-    for t in range(min(2, slices)):
-        start_exchange(t)
+    start_exchange(0)
 
     e_i = e_occ[pairs[z, 0] * 2 + x]
     e_j = e_occ[pairs[z, 1] * 2 + y]
 
     choose(0)
-    for t in range(2, min(4, slices)):
+    for t in range(1, min(3, slices)):
         start_exchange(t)
 
     @pl.loop(0, 2 * (half // 128))
@@ -212,20 +211,15 @@
             near = e_virt[:, pl.ds(pl.multiple_of(tile * half + g * 128, 128), 128)]
             rec[tile, at, g * 128 : (g + 1) * 128] = 1.0 / (near + far - e_i - e_j)
 
-    if slices > 1:
-        choose(1)
-    for t in range(4, min(6, slices)):
-        start_exchange(t)
-
-    @pl.loop(0, steps + ready + 1)
+    @pl.loop(0, steps + ready - 3)
     def _(n):
-        for t in range(2, slices):
-
-            @pl.when(n == 2 * planes * (t - 2))
+        for t in range(1, slices):
+
+            @pl.when(n == 2 * planes * (t - 1) + 1)
             def _():
                 choose(t)
-                if t + 4 < slices:
-                    start_exchange(t + 4)
+                if t + 2 < slices:
+                    start_exchange(t + 2)
 
         @pl.when(n < steps)
         def _():
@@ -262,9 +256,9 @@
             for s in range(2):
                 fetch((n - ready) // 8, s).start()
 
-        @pl.when((n >= ready + 2) & ((n - ready) % 2 == 0))
-        def _():
-            t, unit = (n - ready - 2) // 8, (n - ready - 2) % 8 // 2
+        @pl.when((n >= ready + 1) & ((n - ready - 1) % 8 < 4))
+        def _():
+            t, unit = (n - ready - 1) // 8, (n - ready - 1) % 8
 
             @pl.when(unit == 0)
             def _():
@@ -275,7 +269,7 @@
             top = pl.multiple_of(unit % 2 * width, 128)
             left = pl.multiple_of((tile + c) % 2 * half, 128)
             lhs = pl.multiple_of(tile * half + unit % 2 * width, 128)
-            turned[...] = held[t % 2, 0, :, :, :, pl.ds(lhs, width)].reshape(2 * planes * rows, width).T
+            turned[...] = held[0, :, :, :, pl.ds(lhs, width)].reshape(2 * planes * rows, width).T
 
             @pl.loop(0, half // 256)
             def _(col):
@@ -283,7 +277,7 @@
                 into = pl.ds(pl.multiple_of(col * 256, 128), 256)
                 acc[tile, pl.ds(top, width), into] += jnp.dot(
                     turned[...],
-                    held[t % 2, 1, :, :, :, cols].reshape(2 * planes * rows, 256),
+                    held[1, :, :, :, cols].reshape(2 * planes * rows, 256),
                     preferred_element_type=jnp.float32,
                 )
 
@@ -349,7 +343,7 @@
     planes = pair_list.shape[0]
     width = virt // 4
     half = virt // 2
-    slices = next(n for n in (5, 3, 2, 1) if local_q % (16 * n) == 0)
+    slices = next(n for n in (3, 2, 1) if local_q % (16 * n) == 0)
     rows = local_q // slices
     steps = 2 * planes * slices
     aux = lax.axis_index("aux")
@@ -378,7 +372,7 @@
             pltpu.VMEM((slices, planes, 2, 2, rows, width), factors.dtype),
             pltpu.VMEM((2, half, half), jnp.float32),
             pltpu.VMEM((2, half, half), jnp.float32),
-            pltpu.VMEM((2, 2, planes, 2, rows, virt), factors.dtype),
+            pltpu.VMEM((2, planes, 2, rows, virt), factors.dtype),
             pltpu.VMEM((width, n_aux * rows), factors.dtype),
             pltpu.VMEM((2, 1, half), jnp.float32),
             pltpu.SemaphoreType.DMA((8,)),
@@ -391,7 +385,7 @@
             pltpu.SemaphoreType.DMA((steps, 3)),
             pltpu.SemaphoreType.DMA((steps,)),
             pltpu.SemaphoreType.DMA((steps,)),
-            pltpu.SemaphoreType.DMA((2, 2)),
+            pltpu.SemaphoreType.DMA((2,)),
         ],
         compiler_params=pltpu.CompilerParams(
             collective_id=0, has_side_effects=True, vmem_limit_bytes=60 * 1024 * 1024

time: 310 us -> 321 us (1.035)
  Pallas kernels: 300 us -> 310 us
    pallas_call x1, Pallas kernels: 300 us -> 310 us  [by_planes(): pl.pallas_call(functools.partial(route, planes, slices), out_shape=[jax.S...]
where the time goes in v7:
time: 321 us; the launch traced here: 320 us
  Pallas kernels  310 us (97%)
  local copies, waits for them, and re-layouts  8.76 us (3%)
    pallas_call x1, Pallas kernels, by_planes(): pl.pallas_call(functools.partial(route, planes, slices), out_shape=[jax.S...  310 us
    unnamed x2, local copies, waits for them, and re-layouts  6.69 us

profile of v7, /device:TPU:1, one launch (start us, length us, event | category | flops | bytes accessed | tf_op | source)
XLA Modules:
  0.0 319.9 jit_solution(17881234709933236584)
XLA Ops:
  0.0 1.3 copy.6.pairs
  1.3 1.3 reshape.6.e_virt
  2.6 5.4 %copy.8 = bf16[480,2,2560]{2,0,1:T(8,128)(2,1)} copy(bf16[480,2,2560]{2,1,0:T(2,128)(2,1)} %param.4) | data formatting | bytes 9830400 | tf_op args[0]
  8.0 309.9 %shard_map.46 = (f32[8,2,1,1280]{3,2,1,0:T(1,128)}, bf16[2,4,2,480,2560]{4,3,2,1,0:T(8,128)(2,1)}, bf16[4,2,480,640]{3,2,1,0:T(8,128)(2,1)}) custom-call(s32[4,2]{1,0:T(4,128)} %copy.6.pairs, f32[8]{0:T(128)} %e_occ.1, f32[1,2560]{1,0:T(1,128)} %reshape.6.e_virt, bf16[2,480,2560]{2,1,0:T(8,128)(2,1)} %bitcast.5), custom_call_target="tpu_custom_call" | custom-call | tf_op jit(solution)/shard_map/pallas_call | solution.py:352
  317.9 1.1 reduce
  319.1 0.1 reshape.7
  319.2 0.1 reduce_sum.9
  319.3 0.7 dynamic-slice_bitcast_fusion
